TPU v7x, 128 devices: a whole 4x4x4 slice. The times are simulated.
128 devices in a mesh: elem: 32 (over y, x, core), mode: 4 (over z).
Axes of the slice: x: 4, y: 4, z: 4, core: 2. Of those that a mesh axis runs over, the one named last changes fastest.
Arguments:
- velocity: float32 [3, 20736, 2, 512], P(None, 'elem', None, 'mode'), may hold values from -3 to 3
- column_width: float32 [32], P('elem'), may hold values from 0.5 to 2
- row_height: float32 [8], replicated, may hold values from 0.5 to 2
- disc_mask: int32 [256], P('elem'), may hold values from 0 to 1, as said below
Outputs:
- velocity_new: float32 [3, 20736, 2, 512], P(None, 'elem', None, 'mode')
Inputs may be any that keep to these rules, and one draw needn't show every extreme that they name: `disc_mask`: in each column of 8 elements the ones form one run of 2 to 4 consecutive rows, counted cyclically in y.
All inputs are finite; a program needn't handle non-finite values.
Results may differ from a plain program's by a relative error of at most 0.0001.
Values sent between devices are 32-bit elements; how exact they have to be, the bound alone decides.
No kernel may reach another device: no remote copies, remote signals or barrier semaphores. Data moves between devices by JAX's collectives and lax.ppermute only.
A program may use at most 128 MiB of HBM per device.

v0:
```python
import functools
import math

import jax
import jax.numpy as jnp
import ml_dtypes
import numpy as np
from jax import lax
from jax.experimental import pallas as pl
from jax.experimental.pallas import tpu as pltpu
from jax.sharding import PartitionSpec as P

ORDER = 8
N1 = ORDER + 1
NN = N1 * N1

gll_points = [
    -1.0,
    -0.8997579954114602,
    -0.6771862795107377,
    -0.3631174638261782,
    0.0,
    0.3631174638261782,
    0.6771862795107377,
    0.8997579954114602,
    1.0,
]
gll_weights = [
    0.0277777777777778,
    0.1654953615608055,
    0.2745387125001617,
    0.3464285109730463,
    0.3715192743764172,
    0.3464285109730463,
    0.2745387125001617,
    0.1654953615608055,
    0.0277777777777778,
]
viscosity = 0.5
time_step = 0.02
thrust_coef = 4.0 / 3.0

MODES = 512
PLANES = 3 * MODES
HALF = PLANES // 2
GROUPS = 4
LOCAL = MODES // GROUPS
ROWS = 8
COLUMNS = 32
CHIPS = COLUMNS // 2
NODES = ROWS * NN
SHARE = NODES // GROUPS
ELEM_ROWS = 2 * NN + 2
BLOCK = 2 * ELEM_ROWS
WIDE = BLOCK // 2
SLOT = NN + 1
PAD = 176
TILE = 256
FORWARD = math.sqrt(MODES) / PLANES
DISC_LO = 3 * PLANES // 8
DISC_HI = 5 * PLANES // 8
VMEM_LIMIT = 24 * 1024 * 1024
F32 = jnp.float32
BF16 = jnp.bfloat16


def derivative_matrix():
    points = np.array(gll_points)
    identity = np.eye(9)
    differences = points[:, None] - points[None, :] + identity
    barycentric = 1.0 / np.prod(differences, axis=1)
    off_diagonal = barycentric[None, :] / barycentric[:, None] / differences * (1.0 - identity)
    return off_diagonal - identity * off_diagonal.sum(axis=1)[:, None]


W1 = np.array(gll_weights)
D1 = derivative_matrix()
K1 = (D1.T @ (W1[:, None] * D1)) / W1[:, None]
MULT = np.ones(9)
MULT[0] = MULT[8] = 0.5


def split_table(table):
    table = np.asarray(table, np.float32)
    high = table.astype(ml_dtypes.bfloat16)
    low = (table - high.astype(np.float32)).astype(ml_dtypes.bfloat16)
    return high, low


def plane_tables():
    k = np.arange(MODES)[:, None]
    j = np.arange(HALF)[None, :]
    angle = 2.0 * np.pi / PLANES * ((k * j) % PLANES)
    return [jnp.asarray(t) for t in split_table(np.cos(angle)) + split_table(np.sin(angle))]


def two_elements(matrix):
    table = np.zeros((PAD, PAD))
    for e in range(2):
        at = slice(e * SLOT, e * SLOT + NN)
        table[at, at] = matrix
    return table


def gradient_table():
    one = np.eye(9)
    table = np.concatenate(
        [-two_elements(np.kron(D1, one)), -two_elements(np.kron(one, D1))], axis=0
    )
    return jnp.asarray(np.concatenate(split_table(table), axis=0))


def mode_table():
    k = np.arange(MODES)
    weight = np.where(k == 0, 1.0, 2.0) / math.sqrt(MODES)
    table = np.zeros((8, MODES), np.float32)
    table[0] = weight
    table[1] = weight * 8.0 * k / MODES
    table[2] = (-1.0) ** k - 1.0
    return jnp.asarray(table)


def node_table():
    table = np.zeros((PAD, 128), np.float32)
    for e in range(2):
        table[e * SLOT : e * SLOT + NN] = np.kron(W1, W1)[:, None]
    return jnp.asarray(table)


def device_mode_table():
    k = np.arange(MODES)
    j = np.arange(DISC_LO, DISC_HI)[:, None]
    angle = 2.0 * np.pi / PLANES * ((k[None, :] * j) % PLANES)
    kz = 8.0 * k / MODES
    rows = np.zeros((8, MODES))
    rows[0] = FORWARD * np.cos(angle).sum(axis=0)
    rows[1] = -FORWARD * np.sin(angle).sum(axis=0)
    rows[2] = 1.0 / time_step + viscosity * kz * kz
    table = rows.reshape(8, GROUPS, LOCAL).transpose(1, 0, 2)
    return jnp.asarray(table.astype(np.float32))


def split(value):
    high = value.astype(BF16)
    return jnp.concatenate([high, (value - high.astype(F32)).astype(BF16)], axis=0)


def dot(left, right, transposed=False):
    dims = (((1,), (1 if transposed else 0,)), ((), ()))
    return lax.dot_general(left, right, dims, preferred_element_type=F32)


def dot3(left, right, transposed=False):
    rows = left.shape[0] // 2
    both = dot(left, right[0], transposed)
    return both[:rows] + (both[rows:] + dot(left[:rows], right[1], transposed))


def block_lanes(distance):
    source = lax.rem(lax.axis_index("mode") + GROUPS - distance, GROUPS)
    return pl.ds(pl.multiple_of(source * LOCAL, LOCAL), LOCAL)


def pack_kernel(v_ref, *out_refs):
    me = lax.axis_index("mode")
    for c in range(v_ref.shape[0]):
        for d in range(GROUPS):
            target = lax.rem(me + d, GROUPS)
            for e in range(2):
                base = c * BLOCK + e * ELEM_ROWS
                out_refs[d][pl.ds(base, 2 * NN), :] = v_ref[
                    c, pl.ds((2 * target + e) * 2 * NN, 2 * NN), :
                ]
                out_refs[d][pl.ds(base + 2 * NN, 2), :] = jnp.zeros((2, LOCAL), F32)


def plane_tile(t):
    columns = pl.ds(pl.multiple_of(t * TILE, TILE), TILE)
    plane = lax.broadcasted_iota(jnp.int32, (1, TILE), 1) + t * TILE
    return columns, plane


def element_values(ref):
    me = lax.axis_index("mode")
    first = lax.broadcasted_iota(jnp.int32, (PAD, 1), 0) < SLOT
    return jnp.where(first, ref[2 * me].astype(F32), ref[2 * me + 1].astype(F32))


def load_modes(v_refs, modes_ref, a_ref, b_ref, components):
    zeros = jnp.zeros((PAD - WIDE, LOCAL), F32)
    extra = jnp.zeros((components * 2 * PAD, LOCAL), F32)
    for d, v_ref in enumerate(v_refs):
        lanes = block_lanes(d)
        weight = modes_ref[0:1, lanes]
        wave = modes_ref[1:2, lanes]
        a, b = [], []
        for c in range(components):
            re = v_ref[pl.ds(c * BLOCK, WIDE, stride=2), :]
            im = v_ref[pl.ds(c * BLOCK + 1, WIDE, stride=2), :]
            a += [re * weight, zeros, im * wave, zeros]
            b += [im * weight, zeros, re * wave, zeros]
        a = jnp.concatenate(a, axis=0)
        extra = extra + a * modes_ref[2:3, lanes]
        a_ref[:, lanes] = split(a)
        b_ref[:, lanes] = split(jnp.concatenate(b, axis=0))
    return jnp.sum(extra, axis=1, keepdims=True)


def plane_values(t, a_ref, b_ref, cos, sin, extra):
    _, plane = plane_tile(t)
    even = dot3(a_ref[...], cos)
    odd = dot3(b_ref[...], sin)
    result = []
    for c in range(extra.shape[0] // (2 * PAD)):
        u = slice(2 * c * PAD, (2 * c + 1) * PAD)
        z = slice((2 * c + 1) * PAD, (2 * c + 2) * PAD)
        field = [even[u] - odd[u], even[u] + odd[u]]
        along = [even[z] + odd[z], even[z] - odd[z]]
        if t == 0:
            start = (plane == 0).astype(F32)
            field[1] = field[1] + extra[u] * start
            along[1] = along[1] + extra[z] * start
        result.append((field, along))
    return result


def slope_terms(gradient_ref, field, push_x, push_y):
    high = field.astype(BF16)
    slopes = dot3(gradient_ref[...], (high, (field - high.astype(F32)).astype(BF16)))
    return push_x * slopes[:PAD] + push_y * slopes[PAD:]


def slope_scales(width_ref, height_ref):
    return 2.0 / jnp.full((PAD, 1), width_ref[0]), 2.0 / element_values(height_ref)


def add_modes(t, tends, cos, sin, modes_ref, re_ref, im_ref):
    gather = lambda values: split(jnp.concatenate(values, axis=0))
    re = dot3(gather([low + high for low, high in tends]), cos, True)
    im = dot3(gather([low - high for low, high in tends]), sin, True)
    if t == 0:
        last = jnp.concatenate([high[:, 0:1] for _, high in tends], axis=0)
        re_ref[...] = re + last * modes_ref[2:3, :]
        im_ref[...] = im
    else:
        re_ref[...] += re
        im_ref[...] += im


def store_modes(re_ref, im_ref, out_refs):
    for d in range(GROUPS):
        target = lax.rem(lax.axis_index("mode") + d, GROUPS)
        lanes = pl.ds(pl.multiple_of(target * LOCAL, LOCAL), LOCAL)
        for c in range(re_ref.shape[0] // PAD):
            rows = pl.ds(c * PAD, WIDE)
            out_refs[d][pl.ds(c * BLOCK, WIDE, stride=2), :] = FORWARD * re_ref[rows, lanes]
            out_refs[d][pl.ds(c * BLOCK + 1, WIDE, stride=2), :] = -FORWARD * im_ref[rows, lanes]


def first_kernel(
    width_ref, height_ref, disc_ref, v0_ref, v1_ref, v2_ref, v3_ref,
    ch_ref, cl_ref, sh_ref, sl_ref, gradient_ref, modes_ref, nodes_ref,
    field_ref, along_ref, tend_ref, press_ref, a_ref, b_ref,
):
    extra = load_modes((v0_ref, v1_ref, v2_ref, v3_ref), modes_ref, a_ref, b_ref, 2)
    scale_x, scale_y = slope_scales(width_ref, height_ref)
    heights = element_values(height_ref)
    weight = element_values(disc_ref) * (width_ref[0] * heights / 4.0) * nodes_ref[:, 0:1]
    press_ref[...] = jnp.zeros_like(press_ref)
    for t in range(HALF // TILE):
        columns, plane = plane_tile(t)
        cos = (ch_ref[:, columns], cl_ref[:, columns])
        sin = (sh_ref[:, columns], sl_ref[:, columns])
        values = plane_values(t, a_ref, b_ref, cos, sin, extra)
        for side in range(2):
            push_x = values[0][0][side] * scale_x
            push_y = values[1][0][side] * scale_y
            for c, (field, along) in enumerate(values):
                field_ref[c, side, :, columns] = field[side]
                along_ref[c, side, :, columns] = along[side]
                tend_ref[c, side, :, columns] = slope_terms(
                    gradient_ref, field[side], push_x, push_y
                )
        low, high = values[0][0]
        in_low = (plane >= DISC_LO).astype(F32)
        in_high = ((plane > PLANES - DISC_HI) | (plane == 0)).astype(F32)
        share = weight * (low * low * in_low + high * high * in_high)
        share = jnp.sum(share.reshape(PAD // 8, 8, TILE), axis=0)
        press_ref[...] += share[:, :128] + share[:, 128:]


def second_kernel(
    v0_ref, v1_ref, v2_ref, v3_ref, along01_ref, tend_ref, press_ref,
    ch_ref, cl_ref, sh_ref, sl_ref, modes_ref,
    field_ref, along_ref, o0_ref, o1_ref, o2_ref, o3_ref, a_ref, b_ref, re_ref, im_ref,
):
    out_refs = (o0_ref, o1_ref, o2_ref, o3_ref)
    extra = load_modes((v0_ref, v1_ref, v2_ref, v3_ref), modes_ref, a_ref, b_ref, 1)
    for t in range(HALF // TILE):
        columns, _ = plane_tile(t)
        cos = (ch_ref[:, columns], cl_ref[:, columns])
        sin = (sh_ref[:, columns], sl_ref[:, columns])
        ((field, along),) = plane_values(t, a_ref, b_ref, cos, sin, extra)
        tends = [[None, None], [None, None]]
        for side in range(2):
            field_ref[side, :, columns] = field[side]
            along_ref[side, :, columns] = along[side]
            for c in range(2):
                tends[c][side] = (
                    tend_ref[c, side, :, columns] + field[side] * along01_ref[c, side, :, columns]
                )
        add_modes(t, tends, cos, sin, modes_ref, re_ref, im_ref)
    store_modes(re_ref, im_ref, out_refs)
    for out_ref in out_refs:
        out_ref[pl.ds(2 * NN, 1), :] = jnp.sum(press_ref[...], axis=0, keepdims=True)


def choose_edges(values, inner_ref, outer_ref, at):
    even = lax.rem(lax.axis_index("elem"), 2) == 0
    first, last = values
    inner_ref[at] = jnp.where(even, last, first)
    outer_ref[at] = jnp.where(even, first, last)


def edge_rows(side, part, element):
    return pl.ds((2 * part + element) * N1, N1), element * SLOT + side * (NN - N1)


def third_kernel(
    width_ref, height_ref, field01_ref, field_ref, along_ref, v0_ref, v1_ref, v2_ref, v3_ref,
    ch_ref, cl_ref, sh_ref, sl_ref, gradient_ref, modes_ref,
    re_ref, im_ref, inner_ref, outer_ref, first_ref, last_ref,
):
    scale_x, scale_y = slope_scales(width_ref, height_ref)
    for t in range(HALF // TILE):
        columns, _ = plane_tile(t)
        cos = (ch_ref[:, columns], cl_ref[:, columns])
        sin = (sh_ref[:, columns], sl_ref[:, columns])
        tends = []
        for side in range(2):
            field = field_ref[side, :, columns]
            push_x = field01_ref[0, side, :, columns] * scale_x
            push_y = field01_ref[1, side, :, columns] * scale_y
            tends.append(
                slope_terms(gradient_ref, field, push_x, push_y)
                + field * along_ref[side, :, columns]
            )
        add_modes(t, [tends], cos, sin, modes_ref, re_ref, im_ref)
    for side, edge_ref in enumerate((first_ref, last_ref)):
        edge_ref[...] = jnp.zeros_like(edge_ref)
        for p in range(2):
            for e in range(2):
                rows, start = edge_rows(side, p, e)
                for d, v_ref in enumerate((v0_ref, v1_ref, v2_ref, v3_ref)):
                    edge_ref[rows, block_lanes(d)] = v_ref[pl.ds(2 * start + p, N1, stride=2), :]
                tend = FORWARD * re_ref[pl.ds(start, N1), :] if p == 0 else (
                    -FORWARD * im_ref[pl.ds(start, N1), :]
                )
                edge_ref[rows, :] = (edge_ref[rows, :] * (1.0 / time_step) + tend) * width_ref[0]
    choose_edges((first_ref[...], last_ref[...]), inner_ref, outer_ref, ...)


def fourth_kernel(
    width_ref, re_ref, im_ref, from_inner_ref, from_outer_ref,
    o0_ref, o1_ref, o2_ref, o3_ref, re_sum_ref, im_sum_ref,
):
    even = lax.rem(lax.axis_index("elem"), 2) == 0
    re_sum_ref[...] = re_ref[...]
    im_sum_ref[...] = im_ref[...]
    scale = 1.0 / (FORWARD * jnp.full((N1, MODES), width_ref[0]))
    for side in range(2):
        for p in range(2):
            for e in range(2):
                rows, start = edge_rows(side, p, e)
                inner, outer = from_inner_ref[rows, :], from_outer_ref[rows, :]
                edge = jnp.where(even, inner, outer) if side else jnp.where(even, outer, inner)
                if p == 0:
                    re_sum_ref[pl.ds(start, N1), :] += edge * scale
                else:
                    im_sum_ref[pl.ds(start, N1), :] -= edge * scale
    store_modes(re_sum_ref, im_sum_ref, (o0_ref, o1_ref, o2_ref, o3_ref))


def row_values(height_ref):
    row = lax.broadcasted_iota(jnp.int32, (ROWS, 128), 0)
    value = jnp.zeros((ROWS, 128), F32)
    for r in range(ROWS):
        value = jnp.where(row == r, height_ref[r].astype(F32), value)
    return value


def next_row(value):
    return jnp.roll(value, -1, axis=0)


def right_side(thrusted, width_ref, height_ref, disc_ref, v_ref, blocks, table_ref, b_ref, t_ref):
    me = lax.axis_index("mode")
    heights = row_values(height_ref)
    width = jnp.full((ROWS, 128), width_ref[0])
    if thrusted:
        disc = row_values(disc_ref)
        total = sum(ref[2 * NN : 2 * NN + 1, :] for ref in blocks)
        total = jnp.sum(total, axis=1, keepdims=True)
        area = (DISC_HI - DISC_LO) * width * jnp.sum(disc * heights, axis=0, keepdims=True)
        thrust = -(0.5 * thrust_coef * ORDER) * (total / area) / width * disc
    jacobian = width * heights / 4.0
    for c in range(v_ref.shape[0]):
        for d, block_ref in enumerate(blocks):
            source = lax.rem(me + GROUPS - d, GROUPS)
            rows = pl.ds(pl.multiple_of(source * BLOCK, 8), BLOCK)
            t_ref[c, rows, :] = block_ref[pl.ds(c * BLOCK, BLOCK), :]
    for c in range(v_ref.shape[0]):
        for p in range(2):
            q = 2 * c + p
            push = thrust * table_ref[me, p : p + 1, :] if thrusted and c == 0 else None

            def value(a, b):
                at = (a * N1 + b) * 2 + p
                node = v_ref[c, pl.ds(at, ROWS, stride=2 * NN), :] * (1.0 / time_step)
                node = node + t_ref[c, pl.ds(at, ROWS, stride=ELEM_ROWS), :]
                if push is not None:
                    node = node + push
                return node * (jacobian * float(W1[a] * W1[b]))

            for a in range(N1):
                upper = value(a, N1 - 1) + next_row(value(a, 0))
                lower = jnp.roll(upper, 1, axis=0)
                for b in range(N1):
                    node = lower if b == 0 else upper if b == N1 - 1 else value(a, b)
                    b_ref[q, a * N1 + b] = node


def choose_all_edges(x_ref, inner_ref, outer_ref, q):
    for b in range(N1 - 1):
        ends = x_ref[q, b], x_ref[q, (N1 - 1) * N1 + b]
        choose_edges(ends, inner_ref, outer_ref, (q, b))


def right_kernel(
    width_ref, height_ref, disc_ref, v_ref, t0_ref, t1_ref, t2_ref, t3_ref, table_ref,
    b_ref, inner_ref, outer_ref, t_ref,
):
    blocks = (t0_ref, t1_ref, t2_ref, t3_ref)
    right_side(True, width_ref, height_ref, disc_ref, v_ref, blocks, table_ref, b_ref, t_ref)
    for q in range(b_ref.shape[0]):
        choose_all_edges(b_ref, inner_ref, outer_ref, q)


def add_edges(x_ref, inner_ref, outer_ref, q, store_ref):
    even = lax.rem(lax.axis_index("elem"), 2) == 0
    for a in range(1, N1 - 1):
        for b in range(N1):
            store_ref[q, a * N1 + b] = x_ref[q, a * N1 + b]
    for b in range(N1 - 1):
        inner, outer = inner_ref[q, b], outer_ref[q, b]
        for a, edge in ((0, jnp.where(even, outer, inner)), (N1 - 1, jnp.where(even, inner, outer))):
            store_ref[q, a * N1 + b] = x_ref[q, a * N1 + b] + edge
            if b == 0:
                n = a * N1 + N1 - 1
                store_ref[q, n] = x_ref[q, n] + next_row(edge)


def stiff_line(values):
    half = N1 // 2
    even = [values[i] + values[N1 - 1 - i] for i in range(half)] + [values[half]]
    odd = [values[i] - values[N1 - 1 - i] for i in range(half)]
    result = [None] * N1
    for i in range(half + 1):
        total = even[half] * float(K1[i, half])
        for j in range(half):
            total = total + even[j] * float(0.5 * (K1[i, j] + K1[i, N1 - 1 - j]))
        if i == half:
            result[i] = total
        else:
            rest = odd[0] * float(0.5 * (K1[i, 0] - K1[i, N1 - 1]))
            for j in range(1, half):
                rest = rest + odd[j] * float(0.5 * (K1[i, j] - K1[i, N1 - 1 - j]))
            result[i] = total + rest
            result[N1 - 1 - i] = total - rest
    return result


def operator_scales(width_ref, height_ref, table_ref):
    me = lax.axis_index("mode")
    heights = row_values(height_ref)
    width = jnp.full((ROWS, 128), width_ref[0])
    mass = width * heights / 4.0 * table_ref[me, 2:3, :]
    return mass, viscosity * heights / width, viscosity * width / heights


def local_operator(x_ref, q, scratch_ref, scales, emit):
    mass, ratio_x, ratio_y = scales
    for b in range(N1):
        values = [x_ref[q, a * N1 + b] for a in range(N1)]
        for a, stiff in enumerate(stiff_line(values)):
            scratch_ref[a * N1 + b] = mass * values[a] + ratio_x * stiff
    for a in range(N1):
        values = [x_ref[q, a * N1 + b] for b in range(N1)]
        stiff = stiff_line(values)
        emit(
            a,
            values,
            [
                (scratch_ref[a * N1 + b] + ratio_y * stiff[b]) * float(W1[a] * W1[b])
                for b in range(N1)
            ],
        )


def image_side(scales, b_ref, w_ref, inner_ref, outer_ref, sums_ref, scratch_ref, q):
    state = [jnp.zeros((ROWS, 128), F32), jnp.zeros((ROWS, 128), F32)]

    def emit(a, values, image):
        for b in range(N1):
            state[0] = state[0] + values[b] * values[b] * float(MULT[a] * MULT[b])
            state[1] = state[1] + values[b] * image[b]
        upper = image[N1 - 1] + next_row(image[0])
        lower = jnp.roll(upper, 1, axis=0)
        for b in range(N1):
            value = lower if b == 0 else upper if b == N1 - 1 else image[b]
            w_ref[q, a * N1 + b] = value

    local_operator(b_ref, q, scratch_ref, scales, emit)
    choose_all_edges(w_ref, inner_ref, outer_ref, q)
    sums_ref[q, 0] = state[0]
    sums_ref[q, 1] = state[1]


def image_kernel(
    width_ref, height_ref, x_ref, from_inner_ref, from_outer_ref, table_ref,
    b_ref, w_ref, inner_ref, outer_ref, sums_ref, scratch_ref,
):
    scales = operator_scales(width_ref, height_ref, table_ref)

    def part(q, carry):
        add_edges(x_ref, from_inner_ref, from_outer_ref, q, b_ref)
        image_side(scales, b_ref, w_ref, inner_ref, outer_ref, sums_ref, scratch_ref, q)
        return carry

    lax.fori_loop(0, x_ref.shape[0], part, 0)


def right_image_kernel(
    width_ref, height_ref, v_ref, t0_ref, t1_ref, t2_ref, t3_ref, table_ref,
    b_ref, w_ref, inner_ref, outer_ref, sums_ref, t_ref, scratch_ref,
):
    blocks = (t0_ref, t1_ref, t2_ref, t3_ref)
    right_side(False, width_ref, height_ref, None, v_ref, blocks, table_ref, b_ref, t_ref)
    scales = operator_scales(width_ref, height_ref, table_ref)

    def part(q, carry):
        image_side(scales, b_ref, w_ref, inner_ref, outer_ref, sums_ref, scratch_ref, q)
        return carry

    lax.fori_loop(0, b_ref.shape[0], part, 0)


def whole(value):
    return jnp.sum(value, axis=0, keepdims=True)


def products_kernel(
    start, chained, width_ref, height_ref, x_ref, from_inner_ref, from_outer_ref, b_ref, sums_ref, table_ref,
    *rest,
):
    g_ref, out_ref, scratch_ref = rest[-3:]
    scales = operator_scales(width_ref, height_ref, table_ref)
    out_ref[...] = rest[0][...] if chained else jnp.zeros_like(out_ref)

    def part(q, carry):
        add_edges(x_ref, from_inner_ref, from_outer_ref, q, g_ref)
        cross = jnp.zeros((ROWS, 128), F32)
        for n in range(NN):
            cross = cross + b_ref[q, n] * g_ref[q, n] * float(MULT[n // N1] * MULT[n % N1])
        norm = whole(sums_ref[q, 0])
        shift = jnp.where(norm > 0, whole(cross) / norm, 0.0)
        for n in range(NN):
            g_ref[q, n] = g_ref[q, n] - shift * b_ref[q, n]
        state = [jnp.zeros((ROWS, 128), F32) for _ in range(3)]

        def emit(a, values, image):
            for b in range(N1):
                state[0] = state[0] + values[b] * values[b] * float(MULT[a] * MULT[b])
                state[1] = state[1] + values[b] * image[b]
                state[2] = state[2] + b_ref[q, a * N1 + b] * image[b]

        local_operator(g_ref, q, scratch_ref, scales, emit)
        rows = [norm, shift] + [whole(value) for value in state] + [whole(sums_ref[q, 1])]
        for i, row in enumerate(rows):
            out_ref[pl.ds(6 * i + start + q, 1), :] = row
        return carry

    lax.fori_loop(0, x_ref.shape[0], part, 0)


def merged(blocks):
    norm = sum(block[0] for block in blocks)
    shift = sum(block[0] * block[1] for block in blocks) / norm
    shift = jnp.where(norm > 0, shift, 0.0)
    rest, bend, mixed = 0.0, 0.0, 0.0
    for block in blocks:
        gap = block[1] - shift
        rest = rest + (block[2] + gap * gap * block[0])
        bend = bend + (block[3] + gap * (2.0 * block[4] + gap * block[5]))
        mixed = mixed + (block[4] + gap * block[5])
    return norm, shift, rest, bend, mixed, sum(block[5] for block in blocks)


def six(read):
    return [read(pl.ds(6 * i, 6)) for i in range(6)]


def merge_kernel(own_ref, other_ref, out_ref):
    rows = merged([six(lambda at: ref[at, :]) for ref in (own_ref, other_ref)])
    rows = jnp.concatenate(list(rows) + [jnp.zeros((4, 128), F32)], axis=0)
    for d in range(CHIPS):
        out_ref[d] = rows


def update_kernel(own_ref, all_ref, b01_ref, g01_ref, b2_ref, g2_ref, out_ref):
    norm, sigma, rest, bend, _, _ = merged(
        [six(lambda at: all_ref[d, at, :]) for d in range(CHIPS)]
    )
    step = 1.0 / sigma
    norm_next = step * step * rest
    beta = norm_next / norm
    second = norm_next / (step * step * bend - beta * norm_next / step)
    gap = own_ref[pl.ds(6, 6), :] - sigma
    on_b = step + second * (beta - step * gap)
    on_g = -second * step
    for c in range(3):
        b_ref, g_ref = (b01_ref, g01_ref) if c < 2 else (b2_ref, g2_ref)
        for p in range(2):
            q = 2 * c + p
            r = q if c < 2 else p
            left, right = on_b[q : q + 1], on_g[q : q + 1]
            for n in range(NN):
                out_ref[c, pl.ds(2 * n + p, ROWS, stride=2 * NN), :] = (
                    left * b_ref[r, n] + right * g_ref[r, n]
                )


def vmem():
    return pl.BlockSpec(memory_space=pltpu.VMEM)


def smem():
    return pl.BlockSpec(memory_space=pltpu.SMEM)


def component_block(start, count):
    return pl.BlockSpec((count, 2 * NODES, LOCAL), lambda i: (start // count, 0, 0))


class Program:
    def __init__(self):
        self.token = None

    def call(self, kernel, specs, outs, scratch, cost, *args, grid=False, after=()):
        def whole_block(shape):
            return pl.BlockSpec(shape, lambda i: (0,) * len(shape)) if grid else vmem()

        if grid:
            specs = [whole_block(a.shape) if s is None else s for s, a in zip(specs, args)]
        else:
            specs = [vmem() if s is None else s for s in specs]
        count = len(args)
        tokens = tuple(after) + (() if self.token is None else (self.token,))
        specs = specs + [pl.BlockSpec(memory_space=pl.ANY)] * len(tokens)
        args = args + tokens
        body = lambda *refs: kernel(*refs[:count], *refs[len(args) :])
        results = pl.pallas_call(
            body,
            grid=(1,) if grid else (),
            in_specs=specs,
            out_specs=[whole_block(shape) for shape in outs],
            out_shape=[jax.ShapeDtypeStruct(shape, F32) for shape in outs],
            scratch_shapes=scratch,
            compiler_params=pltpu.CompilerParams(vmem_limit_bytes=VMEM_LIMIT),
            cost_estimate=pl.CostEstimate(
                flops=int(cost[0]), bytes_accessed=int(cost[1]), transcendentals=0
            ),
        )(*args)
        self.token = results[-1]
        return results


def swap(blocks):
    return [blocks[0]] + [
        lax.ppermute(blocks[d], "mode", [(i, (i + d) % GROUPS) for i in range(GROUPS)])
        for d in range(1, GROUPS)
    ]


def trade(inner, outer):
    pair = [(i, i ^ 1) for i in range(COLUMNS)]
    across = [(i, (i + (1 if i % 2 else -1)) % COLUMNS) for i in range(COLUMNS)]
    return lax.ppermute(inner, "elem", pair), lax.ppermute(outer, "elem", across)


def on_device(velocity, column_width, row_height, disc_mask):
    geometry = (column_width, row_height)
    own = velocity.reshape(3, 2 * NODES, LOCAL)
    table = device_mode_table()
    planes = plane_tables()
    modes = mode_table()
    nodes = node_table()
    gradient = gradient_table()
    run = Program()
    chunks = ((0, 2), (2, 1))

    def block(count):
        return (count * BLOCK, LOCAL)

    def values(count):
        return (count, 2, PAD, HALF) if count > 1 else (2, PAD, HALF)

    def rows_scratch(count):
        return [pltpu.VMEM((count * 4 * PAD, MODES), BF16) for _ in range(2)]

    def modes_scratch(count):
        return [pltpu.VMEM((count * PAD, MODES), F32) for _ in range(2)]

    sent = [
        swap(
            run.call(
                pack_kernel, [component_block(*chunk)], [block(chunk[1])] * GROUPS, [], (1e3, 1e3),
                own, grid=True,
            )
        )
        for chunk in chunks
    ]
    field01, along01, tend01, press = run.call(
        first_kernel,
        [smem()] * 3 + [None] * 11,
        [values(2)] * 3 + [(8, 128)],
        rows_scratch(2),
        (1e3, 1e3),
        *geometry, disc_mask, *sent[0], *planes, gradient, modes, nodes,
    )
    field2, along2, *back01 = run.call(
        second_kernel,
        [None] * 12,
        [values(1)] * 2 + [block(2)] * GROUPS,
        rows_scratch(1) + modes_scratch(2),
        (1e3, 1e3),
        *sent[1], along01, tend01, press, *planes, modes,
    )
    back01 = swap(back01)
    spectrum, edges = (PAD, MODES), (40, MODES)
    re2, im2, *ends = run.call(
        third_kernel,
        [smem()] * 2 + [None] * 13,
        [spectrum, spectrum, edges, edges],
        [pltpu.VMEM(edges, F32), pltpu.VMEM(edges, F32)],
        (1e3, 1e3),
        *geometry, field01, field2, along2, *sent[1], *planes, gradient, modes,
    )
    back2 = swap(
        run.call(
            fourth_kernel,
            [smem()] + [None] * 4,
            [block(1)] * GROUPS,
            modes_scratch(1),
            (1e3, 1e3),
            column_width, re2, im2, *trade(*ends),
            after=back01[1:2],
        )
    )
    scratch = [pltpu.VMEM((NN, ROWS, LOCAL), F32)]
    part, rights, gaps, sums = {}, {}, {}, {}

    def field(count):
        return (2 * count, NN, ROWS, LOCAL)

    def edge(count):
        return (2 * count, N1 - 1, ROWS, LOCAL)

    def right(i, back, after):
        start, count = chunks[i]
        x, *edges = run.call(
            right_kernel,
            [smem()] * 3 + [component_block(start, count)] + [None] * 5,
            [field(count), edge(count), edge(count)],
            [pltpu.VMEM((count, ROWS * ELEM_ROWS, LOCAL), F32)],
            (1e3, 1e3),
            *geometry, disc_mask, own, *back, table,
            grid=True,
            after=after,
        )
        part[i] = (x, *trade(*edges))

    def right_image(i, back):
        start, count = chunks[i]
        rights[i], x, *edges, sums[i] = run.call(
            right_image_kernel,
            [smem()] * 2 + [component_block(start, count)] + [None] * 5,
            [field(count), field(count), edge(count), edge(count), (2 * count, 2, ROWS, LOCAL)],
            [pltpu.VMEM((count, ROWS * ELEM_ROWS, LOCAL), F32)] + scratch,
            (1e3, 1e3),
            *geometry, own, *back, table,
            grid=True,
        )
        part[i] = (x, *trade(*edges))

    def image(i):
        count = chunks[i][1]
        rights[i], x, *edges, sums[i] = run.call(
            image_kernel,
            [smem()] * 2 + [None] * 4,
            [field(count), field(count), edge(count), edge(count), (2 * count, 2, ROWS, LOCAL)],
            scratch,
            (1e3, 1e3),
            *geometry, *part[i], table,
        )
        part[i] = (x, *trade(*edges))

    def product(i, *before):
        start, count = chunks[i]
        gaps[i], total = run.call(
            functools.partial(products_kernel, 2 * start, len(before) > 0),
            [smem()] * 2 + [None] * (6 + len(before)),
            [field(count), (40, LOCAL)],
            scratch,
            (1e3, 1e3),
            *geometry, *part[i], rights[i], sums[i], table, *before,
        )
        return total

    right(0, back01, ())
    image(0)
    right_image(1, back2)
    total = product(0)
    total = product(1, total)
    other = lax.ppermute(total, "elem", [(i, i ^ 1) for i in range(COLUMNS)])
    (spread,) = run.call(
        merge_kernel, [None] * 2, [(CHIPS, 40, LOCAL)], [], (1e3, 1e3), total, other
    )
    everyone = lax.all_to_all(
        spread, "elem", split_axis=0, concat_axis=0, tiled=True,
        axis_index_groups=[[2 * i + core for i in range(CHIPS)] for core in range(2)],
    )
    (result,) = run.call(
        update_kernel,
        [None] * 6,
        [(3, 2 * NODES, LOCAL)],
        [],
        (1e3, 1e3),
        total, everyone, rights[0], gaps[0], rights[1], gaps[1],
    )
    return result.reshape(3, NODES, 2, LOCAL)


def solution(mesh):
    return jax.shard_map(
        on_device,
        mesh=mesh,
        in_specs=(P(None, "elem", None, "mode"), P("elem"), P(), P("elem")),
        out_specs=P(None, "elem", None, "mode"),
        check_vma=False,
    )
```

profile of v0, /device:TPU:1, one launch (start us, length us, event | category | flops | bytes accessed | tf_op | source)
XLA Modules:
  0.0 95.9 jit_solution(9917077109383506299)
XLA Ops:
  0.0 1.6 %copy-done = f32[3,648,2,128]{3,2,1,0:T(2,128)S(1)} copy-done((f32[3,648,2,128]{3,2,1,0:T(2,128)S(1)}, f32[3,648,2,128]{3,2,1,0:T(2,128)}, u32[]{:S(2)}) %copy-start) | copy-done | bytes 1990680
  1.6 0.1 shard_map.118
  1.7 0.0 copy-start.2
  1.7 0.0 copy-start.3
  1.7 0.0 copy-start.6
  1.7 0.0 copy-start.8
  1.7 0.0 copy-start.9
  1.7 0.0 copy-start.10
  1.7 0.0 copy-start.11
  1.8 2.5 %collective-permute-start = (f32[656,128]{1,0:T(8,128)S(1)}, f32[656,128]{1,0:T(8,128)S(1)}, u32[]{:S(2)}, u32[]{:S(2)}) collective-permute-start(f32[656,128]{1,0:T(8,128)S(1)} %get-tuple-element.49), channel_id=1, source_target_pairs={{0,1},{1,2},{2,3},{3,0},{4,5},{5,6},{6,7},{7,4},{8,9},{9,10},{10,1... | collective-permute-start | bytes 1007624 | tf_op jit(solution)/shard_map/ppermute | solution.py:690
  4.3 3.3 %collective-permute-start.1 = (f32[656,128]{1,0:T(8,128)S(1)}, f32[656,128]{1,0:T(8,128)S(1)}, u32[]{:S(2)}, u32[]{:S(2)}) collective-permute-start(f32[656,128]{1,0:T(8,128)S(1)} %get-tuple-element.50), channel_id=1, source_target_pairs={{0,2},{1,3},{2,0},{3,1},{4,6},{5,7},{6,4},{7,5},{8,10},{9,11},{10,... | collective-permute-start | bytes 1007624 | tf_op jit(solution)/shard_map/ppermute | solution.py:690
  7.6 0.7 collective-permute-start.2
  8.4 0.8 collective-permute-start.3
  9.2 0.4 collective-permute-start.4
  9.6 4.4 %collective-permute-done.refs_4_ = f32[656,128]{1,0:T(8,128)S(1)} collective-permute-done((f32[656,128]{1,0:T(8,128)S(1)}, f32[656,128]{1,0:T(8,128)S(1)}, u32[]{:S(2)}, u32[]{:S(2)}) %collective-permute-start) | collective-permute-done | bytes 335904 | tf_op jit(solution)/shard_map/ppermute | solution.py:690
  14.0 1.1 %collective-permute-start.5 = (f32[328,128]{1,0:T(8,128)S(1)}, f32[328,128]{1,0:T(8,128)S(1)}, u32[]{:S(2)}, u32[]{:S(2)}) collective-permute-start(f32[328,128]{1,0:T(8,128)S(1)} %get-tuple-element.52.refs_14_), channel_id=1, source_target_pairs={{0,3},{1,0},{2,1},{3,2},{4,7},{5,4},{6,5},{7,6},{8,11},{9,8},{10,9... | collective-permute-start | bytes 503816 | tf_op jit(solution)/shard_map/ppermute | solution.py:690
  15.8 6.3 %collective-permute-done.1.refs_5_ = f32[656,128]{1,0:T(8,128)S(1)} collective-permute-done((f32[656,128]{1,0:T(8,128)S(1)}, f32[656,128]{1,0:T(8,128)S(1)}, u32[]{:S(2)}, u32[]{:S(2)}) %collective-permute-start.1) | collective-permute-done | bytes 335904 | tf_op jit(solution)/shard_map/ppermute | solution.py:690
  22.2 6.7 %shard_map.120 = (f32[2,2,176,768]{3,2,1,0:T(8,128)S(1)}, f32[2,2,176,768]{3,2,1,0:T(8,128)S(1)}, f32[2,2,176,768]{3,2,1,0:T(8,128)S(1)}, f32[8,128]{1,0:T(8,128)S(1)}) custom-call(f32[1]{0:T(128)S(6)} %copy.13.refs_0_, f32[8]{0:T(128)S(1)} %copy-done.10, s32[8]{0:T(128)S(1)} %copy-done.11, f32[656,128]{1,0:T(8,128)S(1)} %get-tuple-element.48.refs_3_, ...), custom_call_target="tpu_custom_call" | custom-call | flops 1000 | bytes 1000 | tf_op jit(solution)/shard_map/pallas_call | solution.py:672
  28.9 0.0 collective-permute-done.3.refs_1_.refs_6_
  28.9 0.4 collective-permute-done.4.refs_2_.refs_7_
  29.3 0.0 collective-permute-done.5.refs_3_.refs_8_
  29.3 4.5 %shard_map.121 = (f32[2,176,768]{2,1,0:T(8,128)S(1)}, f32[2,176,768]{2,1,0:T(8,128)S(1)}, f32[656,128]{1,0:T(8,128)S(1)}, f32[656,128]{1,0:T(8,128)S(1)}, f32[65...) custom-call(f32[328,128]{1,0:T(8,128)S(1)} %get-tuple-element.54.refs_0_.refs_5_, ...), custom_call_target="tpu_custom_call" | custom-call | flops 1000 | bytes 1000 | tf_op jit(solution)/shard_map/pallas_call | solution.py:672
  33.8 1.7 %collective-permute-start.8 = (f32[656,128]{1,0:T(8,128)S(1)}, f32[656,128]{1,0:T(8,128)S(1)}, u32[]{:S(2)}, u32[]{:S(2)}) collective-permute-start(f32[656,128]{1,0:T(8,128)S(1)} %get-tuple-element.67), channel_id=1, source_target_pairs={{0,1},{1,2},{2,3},{3,0},{4,5},{5,6},{6,7},{7,4},{8,9},{9,10},{10,1... | collective-permute-start | bytes 1007624 | tf_op jit(solution)/shard_map/ppermute | solution.py:690
  35.5 3.1 %collective-permute-start.12 = (f32[656,128]{1,0:T(8,128)S(1)}, f32[656,128]{1,0:T(8,128)S(1)}, u32[]{:S(2)}, u32[]{:S(2)}) collective-permute-start(f32[656,128]{1,0:T(8,128)S(1)} %get-tuple-element.73), channel_id=1, source_target_pairs={{0,2},{1,3},{2,0},{3,1},{4,6},{5,7},{6,4},{7,5},{8,10},{9,11},{10,... | collective-permute-start | bytes 1007624 | tf_op jit(solution)/shard_map/ppermute | solution.py:690
  38.6 0.0 collective-permute-start.13
  38.6 3.1 %shard_map.122 = (f32[176,512]{1,0:T(8,128)S(1)}, f32[176,512]{1,0:T(8,128)S(1)}, f32[40,512]{1,0:T(8,128)S(1)}, f32[40,512]{1,0:T(8,128)S(1)}) custom-call(f32[1]{0:T(128)S(6)} %copy.13.refs_0_, f32[8]{0:T(128)S(1)} %copy-done.10, f32[2,2,176,768]{3,2,1,0:T(8,128)S(1)} %get-tuple-element.53.refs_2_, f32[2,176,768]{2,1,0:T(8,128)S(1)} %get-tuple-element.60.refs_3_, ...), custom_call_target="tpu_custom_call" | custom-call | flops 1000 | bytes 1000 | tf_op jit(solution)/shard_map/pallas_call | solution.py:672
  41.7 3.1 %collective-permute-start.6 = (f32[40,512]{1,0:T(8,128)S(1)}, f32[40,512]{1,0:T(8,128)S(1)}, u32[]{:S(2)}, u32[]{:S(2)}) collective-permute-start(f32[40,512]{1,0:T(8,128)S(1)} %get-tuple-element.65), channel_id=1, source_target_pairs={{0,4},{4,0},{8,12},{12,8},{16,20},{20,16},{24,28},{28,24},{32,36},... | collective-permute-start | bytes 245768 | tf_op jit(solution)/shard_map/ppermute | solution.py:698
  44.9 1.2 %collective-permute-start.7 = (f32[40,512]{1,0:T(8,128)S(1)}, f32[40,512]{1,0:T(8,128)S(1)}, u32[]{:S(2)}, u32[]{:S(2)}) collective-permute-start(f32[40,512]{1,0:T(8,128)S(1)} %get-tuple-element.66.refs_6_), channel_id=1, source_target_pairs={{0,124},{4,8},{8,4},{12,16},{16,12},{20,24},{24,20},{28,32},{32,28... | collective-permute-start | bytes 245768 | tf_op jit(solution)/shard_map/ppermute | solution.py:698
  46.1 0.0 collective-permute-done.6.refs_3_
  46.1 3.0 %collective-permute-done.7.refs_4_ = f32[40,512]{1,0:T(8,128)S(1)} collective-permute-done((f32[40,512]{1,0:T(8,128)S(1)}, f32[40,512]{1,0:T(8,128)S(1)}, u32[]{:S(2)}, u32[]{:S(2)}) %collective-permute-start.7) | collective-permute-done | bytes 81952 | tf_op jit(solution)/shard_map/ppermute | solution.py:698
  49.0 0.2 shard_map.123
  49.2 3.8 %collective-permute-done.12.refs_6_ = f32[656,128]{1,0:T(8,128)S(1)} collective-permute-done((f32[656,128]{1,0:T(8,128)S(1)}, f32[656,128]{1,0:T(8,128)S(1)}, u32[]{:S(2)}, u32[]{:S(2)}) %collective-permute-start.12) | collective-permute-done | bytes 335904 | tf_op jit(solution)/shard_map/ppermute | solution.py:690
  53.0 0.9 shard_map.124
  53.9 1.7 %collective-permute-start.14 = (f32[4,8,8,128]{3,2,1,0:T(8,128)S(1)}, f32[4,8,8,128]{3,2,1,0:T(8,128)S(1)}, u32[]{:S(2)}, u32[]{:S(2)}) collective-permute-start(f32[4,8,8,128]{3,2,1,0:T(8,128)S(1)} %get-tuple-element.75), channel_id=1, source_target_pairs={{0,4},{4,0},{8,12},{12,8},{16,20},{20,16},{24,28},{28,24},{32,36},... | collective-permute-start | bytes 393224 | tf_op jit(solution)/shard_map/ppermute | solution.py:698
  55.6 1.2 %collective-permute-start.15 = (f32[4,8,8,128]{3,2,1,0:T(8,128)S(1)}, f32[4,8,8,128]{3,2,1,0:T(8,128)S(1)}, u32[]{:S(2)}, u32[]{:S(2)}) collective-permute-start(f32[4,8,8,128]{3,2,1,0:T(8,128)S(1)} %get-tuple-element.76.refs_6_), channel_id=1, source_target_pairs={{0,124},{4,8},{8,4},{12,16},{16,12},{20,24},{24,20},{28,32},{32,28... | collective-permute-start | bytes 393224 | tf_op jit(solution)/shard_map/ppermute | solution.py:698
  56.8 3.1 %collective-permute-start.10 = (f32[328,128]{1,0:T(8,128)S(1)}, f32[328,128]{1,0:T(8,128)S(1)}, u32[]{:S(2)}, u32[]{:S(2)}) collective-permute-start(f32[328,128]{1,0:T(8,128)S(1)} %get-tuple-element.70), channel_id=1, source_target_pairs={{0,2},{1,3},{2,0},{3,1},{4,6},{5,7},{6,4},{7,5},{8,10},{9,11},{10,... | collective-permute-start | bytes 503816 | tf_op jit(solution)/shard_map/ppermute | solution.py:690
  59.8 0.1 collective-permute-done.15.refs_4_
  60.0 2.0 %shard_map.125 = (f32[4,81,8,128]{3,2,1,0:T(8,128)S(1)}, f32[4,81,8,128]{3,2,1,0:T(8,128)S(1)}, f32[4,8,8,128]{3,2,1,0:T(8,128)S(1)}, f32[4,8,8,128]{3,2,1,0:T(8,128)S(1)}, f32[4,2,8,128]{3,2,1,0:T(8,128)S(1)}) custom-call(f32[1]{0:T(128)S(6)} %copy.13.refs_0_, f32[8]{0:T(128)S(1)} %copy-done.10, f32[4,81,8,128]{3,2,1,0:T(8,128)S(1)} %get-tuple-element.74.refs_2_, ...), custom_call_target="tpu_custom_call" | custom-call | flops 1000 | bytes 1000 | tf_op jit(solution)/shard_map/pallas_call | solution.py:672
  62.0 4.6 %collective-permute-start.18 = (f32[4,8,8,128]{3,2,1,0:T(8,128)S(1)}, f32[4,8,8,128]{3,2,1,0:T(8,128)S(1)}, u32[]{:S(2)}, u32[]{:S(2)}) collective-permute-start(f32[4,8,8,128]{3,2,1,0:T(8,128)S(1)} %get-tuple-element.84), channel_id=1, source_target_pairs={{0,4},{4,0},{8,12},{12,8},{16,20},{20,16},{24,28},{28,24},{32,36},... | collective-permute-start | bytes 393224 | tf_op jit(solution)/shard_map/ppermute | solution.py:698
  66.6 1.4 %shard_map.126 = (f32[2,81,8,128]{3,2,1,0:T(8,128)S(1)}, f32[2,81,8,128]{3,2,1,0:T(8,128)S(1)}, f32[2,8,8,128]{3,2,1,0:T(8,128)S(1)}, f32[2,8,8,128]{3,2,1,0:T(8,128)S(1)}, f32[2,2,8,128]{3,2,1,0:T(8,128)S(1)}) custom-call(f32[1]{0:T(128)S(6)} %copy.13.refs_0_, f32[8]{0:T(128)S(1)} %copy-done.10, f32[3,1296,128]{2,1,0:T(8,128)S(1)} %bitcast.5, ...), custom_call_target="tpu_custom_call" | custom-call | flops 1000 | bytes 1000 | tf_op jit(solution)/shard_map/pallas_call | solution.py:672
  68.0 4.2 %collective-permute-start.16 = (f32[2,8,8,128]{3,2,1,0:T(8,128)S(1)}, f32[2,8,8,128]{3,2,1,0:T(8,128)S(1)}, u32[]{:S(2)}, u32[]{:S(2)}) collective-permute-start(f32[2,8,8,128]{3,2,1,0:T(8,128)S(1)} %get-tuple-element.79), channel_id=1, source_target_pairs={{0,4},{4,0},{8,12},{12,8},{16,20},{20,16},{24,28},{28,24},{32,36},... | collective-permute-start | bytes 196616 | tf_op jit(solution)/shard_map/ppermute | solution.py:698
  72.3 2.6 %shard_map.127 = (f32[4,81,8,128]{3,2,1,0:T(8,128)S(1)}, f32[40,128]{1,0:T(8,128)S(1)}) custom-call(f32[1]{0:T(128)S(6)} %copy.13.refs_0_, f32[8]{0:T(128)S(1)} %copy-done.10, f32[4,81,8,128]{3,2,1,0:T(8,128)S(1)} %get-tuple-element.83.refs_2_, f32[4,8,8,128]{3,2,1,0:T(8,128)S(1)} %collective-permute-done.18.refs_3_, ...), custom_call_target="tpu_custom_call" | custom-call | flops 1000 | bytes 1000 | tf_op jit(solution)/shard_map/pallas_call | solution.py:672
  74.9 1.0 %collective-permute-done.17.refs_4_ = f32[2,8,8,128]{3,2,1,0:T(8,128)S(1)} collective-permute-done((f32[2,8,8,128]{3,2,1,0:T(8,128)S(1)}, f32[2,8,8,128]{3,2,1,0:T(8,128)S(1)}, u32[]{:S(2)}, u32[]{:S(2)}) %collective-permute-start.17) | collective-permute-done | bytes 65568 | tf_op jit(solution)/shard_map/ppermute | solution.py:698
  76.0 1.6 %shard_map.128 = (f32[2,81,8,128]{3,2,1,0:T(8,128)S(1)}, f32[40,128]{1,0:T(8,128)S(1)}) custom-call(f32[1]{0:T(128)S(6)} %copy.13.refs_0_, f32[8]{0:T(128)S(1)} %copy-done.10, f32[2,81,8,128]{3,2,1,0:T(8,128)S(1)} %get-tuple-element.78.refs_2_, f32[2,8,8,128]{3,2,1,0:T(8,128)S(1)} %collective-permute-done.16.refs_3_, ...), custom_call_target="tpu_custom_call" | custom-call | flops 1000 | bytes 1000 | tf_op jit(solution)/shard_map/pallas_call | solution.py:672
  77.6 3.5 %collective-permute-start.20 = (f32[40,128]{1,0:T(8,128)S(1)}, f32[40,128]{1,0:T(8,128)S(1)}, u32[]{:S(2)}, u32[]{:S(2)}) collective-permute-start(f32[40,128]{1,0:T(8,128)S(1)} %get-tuple-element.88.refs_0_.refs_2_), channel_id=1, source_target_pairs={{0,4},{4,0},{8,12},{12,8},{16,20},{20,16},{24,28},{28,24},{32,36},... | collective-permute-start | bytes 61448 | tf_op jit(solution)/shard_map/ppermute | solution.py:835
  81.0 0.8 collective-permute-done.20.refs_1_
  81.9 12.3 %all_to_all.5.refs_1_ = f32[16,40,128]{2,1,0:T(8,128)S(1)} all-to-all(f32[16,40,128]{2,1,0:T(8,128)S(1)} %shard_map.129.refs_6_), channel_id=1, replica_groups={{0,8,16,24,32,40,48,56,64,72,80,88,96,104,112,120},{4,12,20,28,36,44,52..., dimensions={0} | all-to-all | bytes 655360 | tf_op jit(solution)/shard_map/all_to_all | solution.py:839
  94.3 1.7 %shard_map.130 = f32[3,1296,128]{2,1,0:T(8,128)} custom-call(f32[40,128]{1,0:T(8,128)S(1)} %get-tuple-element.88.refs_0_.refs_2_, f32[16,40,128]{2,1,0:T(8,128)S(1)} %all_to_all.5.refs_1_, f32[4,81,8,128]{3,2,1,0:T(8,128)S(1)} %get-tuple-element.86.refs_5_.refs_2_, f32[4,81,8,128]{3,2,1,0:T(8,128)S(1)} %get-tuple-element.89.refs_3_, ...), custom_call_target="tpu_custom_call" | custom-call | flops 1000 | bytes 1000 | tf_op jit(solution)/shard_map/pallas_call | solution.py:672
  (32 shorter events, 0.1 us)
Async XLA Ops:
  0.0 1.6 %copy-start = (f32[3,648,2,128]{3,2,1,0:T(2,128)S(1)}, f32[3,648,2,128]{3,2,1,0:T(2,128)}, u32[]{:S(2)}) copy-start(f32[3,648,2,128]{3,2,1,0:T(2,128)} %param.12) | copy-start | bytes 5971972
  1.6 20.6 %copy-start.4 = (bf16[512,768]{1,0:T(8,128)(2,1)S(1)}, bf16[512,768]{1,0:T(8,128)(2,1)}, u32[]{:S(2)}) copy-start(bf16[512,768]{1,0:T(8,128)(2,1)} %constant.18.clone.refs_8_.refs_10_) | copy-start | bytes 2359300
  1.6 20.6 %copy-start.5 = (bf16[512,768]{1,0:T(8,128)(2,1)S(1)}, bf16[512,768]{1,0:T(8,128)(2,1)}, u32[]{:S(2)}) copy-start(bf16[512,768]{1,0:T(8,128)(2,1)} %constant.17.clone.refs_7_.refs_9_) | copy-start | bytes 2359300
  1.7 20.5 %copy-start.2 = (bf16[512,768]{1,0:T(8,128)(2,1)S(1)}, bf16[512,768]{1,0:T(8,128)(2,1)}, u32[]{:S(2)}) copy-start(bf16[512,768]{1,0:T(8,128)(2,1)} %constant.20.clone.refs_10_.refs_12_) | copy-start | bytes 2359300
  1.7 20.5 %copy-start.3 = (bf16[512,768]{1,0:T(8,128)(2,1)S(1)}, bf16[512,768]{1,0:T(8,128)(2,1)}, u32[]{:S(2)}) copy-start(bf16[512,768]{1,0:T(8,128)(2,1)} %constant.19.clone.refs_9_.refs_11_) | copy-start | bytes 2359300
  1.7 20.5 %copy-start.6 = (bf16[704,176]{1,0:T(8,128)(2,1)S(1)}, bf16[704,176]{1,0:T(8,128)(2,1)}, u32[]{:S(2)}) copy-start(bf16[704,176]{1,0:T(8,128)(2,1)} %constant.23.clone.refs_11_.refs_13_) | copy-start | bytes 743428
  1.7 20.5 %copy-start.8 = (f32[8,512]{1,0:T(8,128)S(1)}, f32[8,512]{1,0:T(8,128)}, u32[]{:S(2)}) copy-start(f32[8,512]{1,0:T(8,128)} %constant.21.clone.refs_12_.refs_11_.refs_14_) | copy-start | bytes 49156
  1.7 20.5 %copy-start.9 = (f32[176,128]{1,0:T(8,128)S(1)}, f32[176,128]{1,0:T(8,128)}, u32[]{:S(2)}) copy-start(f32[176,128]{1,0:T(8,128)} %constant.22.clone.refs_13_) | copy-start | bytes 270340
  1.7 20.5 %copy-start.10 = (f32[8]{0:T(128)S(1)}, f32[8]{0:T(128)}, u32[]{:S(2)}) copy-start(f32[8]{0:T(128)} %refs_1_.13) | copy-start | bytes 100
  1.7 20.5 %copy-start.11 = (s32[8]{0:T(128)S(1)}, s32[8]{0:T(128)}, u32[]{:S(2)}) copy-start(s32[8]{0:T(128)} %refs_2_.3) | copy-start | bytes 100
  1.8 12.3 %collective-permute-start = (f32[656,128]{1,0:T(8,128)S(1)}, f32[656,128]{1,0:T(8,128)S(1)}, u32[]{:S(2)}, u32[]{:S(2)}) collective-permute-start(f32[656,128]{1,0:T(8,128)S(1)} %get-tuple-element.49), channel_id=1, source_target_pairs={{0,1},{1,2},{2,3},{3,0},{4,5},{5,6},{6,7},{7,4},{8,9},{9,10},{10,1... | collective-permute-start | bytes 1007624 | tf_op jit(solution)/shard_map/ppermute | solution.py:690
  4.3 17.8 %collective-permute-start.1 = (f32[656,128]{1,0:T(8,128)S(1)}, f32[656,128]{1,0:T(8,128)S(1)}, u32[]{:S(2)}, u32[]{:S(2)}) collective-permute-start(f32[656,128]{1,0:T(8,128)S(1)} %get-tuple-element.50), channel_id=1, source_target_pairs={{0,2},{1,3},{2,0},{3,1},{4,6},{5,7},{6,4},{7,5},{8,10},{9,11},{10,... | collective-permute-start | bytes 1007624 | tf_op jit(solution)/shard_map/ppermute | solution.py:690
  7.6 14.5 %collective-permute-start.2 = (f32[656,128]{1,0:T(8,128)S(1)}, f32[656,128]{1,0:T(8,128)S(1)}, u32[]{:S(2)}, u32[]{:S(2)}) collective-permute-start(f32[656,128]{1,0:T(8,128)S(1)} %get-tuple-element.51.refs_1_), channel_id=1, source_target_pairs={{0,3},{1,0},{2,1},{3,2},{4,7},{5,4},{6,5},{7,6},{8,11},{9,8},{10,9... | collective-permute-start | bytes 1007624 | tf_op jit(solution)/shard_map/ppermute | solution.py:690
  8.4 20.6 %collective-permute-start.3 = (f32[328,128]{1,0:T(8,128)S(1)}, f32[328,128]{1,0:T(8,128)S(1)}, u32[]{:S(2)}, u32[]{:S(2)}) collective-permute-start(f32[328,128]{1,0:T(8,128)S(1)} %get-tuple-element.55), channel_id=1, source_target_pairs={{0,1},{1,2},{2,3},{3,0},{4,5},{5,6},{6,7},{7,4},{8,9},{9,10},{10,1... | collective-permute-start | bytes 503816 | tf_op jit(solution)/shard_map/ppermute | solution.py:690
  9.2 20.1 %collective-permute-start.4 = (f32[328,128]{1,0:T(8,128)S(1)}, f32[328,128]{1,0:T(8,128)S(1)}, u32[]{:S(2)}, u32[]{:S(2)}) collective-permute-start(f32[328,128]{1,0:T(8,128)S(1)} %get-tuple-element.56), channel_id=1, source_target_pairs={{0,2},{1,3},{2,0},{3,1},{4,6},{5,7},{6,4},{7,5},{8,10},{9,11},{10,... | collective-permute-start | bytes 503816 | tf_op jit(solution)/shard_map/ppermute | solution.py:690
  14.0 15.3 %collective-permute-start.5 = (f32[328,128]{1,0:T(8,128)S(1)}, f32[328,128]{1,0:T(8,128)S(1)}, u32[]{:S(2)}, u32[]{:S(2)}) collective-permute-start(f32[328,128]{1,0:T(8,128)S(1)} %get-tuple-element.52.refs_14_), channel_id=1, source_target_pairs={{0,3},{1,0},{2,1},{3,2},{4,7},{5,4},{6,5},{7,6},{8,11},{9,8},{10,9... | collective-permute-start | bytes 503816 | tf_op jit(solution)/shard_map/ppermute | solution.py:690
  33.8 15.2 %collective-permute-start.8 = (f32[656,128]{1,0:T(8,128)S(1)}, f32[656,128]{1,0:T(8,128)S(1)}, u32[]{:S(2)}, u32[]{:S(2)}) collective-permute-start(f32[656,128]{1,0:T(8,128)S(1)} %get-tuple-element.67), channel_id=1, source_target_pairs={{0,1},{1,2},{2,3},{3,0},{4,5},{5,6},{6,7},{7,4},{8,9},{9,10},{10,1... | collective-permute-start | bytes 1007624 | tf_op jit(solution)/shard_map/ppermute | solution.py:690
  35.5 17.5 %collective-permute-start.12 = (f32[656,128]{1,0:T(8,128)S(1)}, f32[656,128]{1,0:T(8,128)S(1)}, u32[]{:S(2)}, u32[]{:S(2)}) collective-permute-start(f32[656,128]{1,0:T(8,128)S(1)} %get-tuple-element.73), channel_id=1, source_target_pairs={{0,2},{1,3},{2,0},{3,1},{4,6},{5,7},{6,4},{7,5},{8,10},{9,11},{10,... | collective-permute-start | bytes 1007624 | tf_op jit(solution)/shard_map/ppermute | solution.py:690
  38.6 14.4 %collective-permute-start.13 = (f32[656,128]{1,0:T(8,128)S(1)}, f32[656,128]{1,0:T(8,128)S(1)}, u32[]{:S(2)}, u32[]{:S(2)}) collective-permute-start(f32[656,128]{1,0:T(8,128)S(1)} %get-tuple-element.62.refs_15_), channel_id=1, source_target_pairs={{0,3},{1,0},{2,1},{3,2},{4,7},{5,4},{6,5},{7,6},{8,11},{9,8},{10,9... | collective-permute-start | bytes 1007624 | tf_op jit(solution)/shard_map/ppermute | solution.py:690
  38.6 14.4 %copy-start.1 = (f32[3,648,2,128]{3,2,1,0:T(2,128)S(1)}, f32[3,648,2,128]{3,2,1,0:T(2,128)}, u32[]{:S(2)}) copy-start(f32[3,648,2,128]{3,2,1,0:T(2,128)} %param.12) | copy-start | bytes 5971972
  38.6 14.4 %copy-start.7 = (f32[4,8,128]{2,1,0:T(8,128)S(1)}, f32[4,8,128]{2,1,0:T(8,128)}, u32[]{:S(2)}) copy-start(f32[4,8,128]{2,1,0:T(8,128)} %constant.16.clone.refs_8_.refs_5_.refs_7_) | copy-start | bytes 49156
  41.7 4.3 %collective-permute-start.6 = (f32[40,512]{1,0:T(8,128)S(1)}, f32[40,512]{1,0:T(8,128)S(1)}, u32[]{:S(2)}, u32[]{:S(2)}) collective-permute-start(f32[40,512]{1,0:T(8,128)S(1)} %get-tuple-element.65), channel_id=1, source_target_pairs={{0,4},{4,0},{8,12},{12,8},{16,20},{20,16},{24,28},{28,24},{32,36},... | collective-permute-start | bytes 245768 | tf_op jit(solution)/shard_map/ppermute | solution.py:698
  44.9 4.2 %collective-permute-start.7 = (f32[40,512]{1,0:T(8,128)S(1)}, f32[40,512]{1,0:T(8,128)S(1)}, u32[]{:S(2)}, u32[]{:S(2)}) collective-permute-start(f32[40,512]{1,0:T(8,128)S(1)} %get-tuple-element.66.refs_6_), channel_id=1, source_target_pairs={{0,124},{4,8},{8,4},{12,16},{16,12},{20,24},{24,20},{28,32},{32,28... | collective-permute-start | bytes 245768 | tf_op jit(solution)/shard_map/ppermute | solution.py:698
  53.9 6.0 %collective-permute-start.14 = (f32[4,8,8,128]{3,2,1,0:T(8,128)S(1)}, f32[4,8,8,128]{3,2,1,0:T(8,128)S(1)}, u32[]{:S(2)}, u32[]{:S(2)}) collective-permute-start(f32[4,8,8,128]{3,2,1,0:T(8,128)S(1)} %get-tuple-element.75), channel_id=1, source_target_pairs={{0,4},{4,0},{8,12},{12,8},{16,20},{20,16},{24,28},{28,24},{32,36},... | collective-permute-start | bytes 393224 | tf_op jit(solution)/shard_map/ppermute | solution.py:698
  55.6 4.4 %collective-permute-start.15 = (f32[4,8,8,128]{3,2,1,0:T(8,128)S(1)}, f32[4,8,8,128]{3,2,1,0:T(8,128)S(1)}, u32[]{:S(2)}, u32[]{:S(2)}) collective-permute-start(f32[4,8,8,128]{3,2,1,0:T(8,128)S(1)} %get-tuple-element.76.refs_6_), channel_id=1, source_target_pairs={{0,124},{4,8},{8,4},{12,16},{16,12},{20,24},{24,20},{28,32},{32,28... | collective-permute-start | bytes 393224 | tf_op jit(solution)/shard_map/ppermute | solution.py:698
  56.8 9.8 %collective-permute-start.9 = (f32[328,128]{1,0:T(8,128)S(1)}, f32[328,128]{1,0:T(8,128)S(1)}, u32[]{:S(2)}, u32[]{:S(2)}) collective-permute-start(f32[328,128]{1,0:T(8,128)S(1)} %get-tuple-element.69), channel_id=1, source_target_pairs={{0,1},{1,2},{2,3},{3,0},{4,5},{5,6},{6,7},{7,4},{8,9},{9,10},{10,1... | collective-permute-start | bytes 503816 | tf_op jit(solution)/shard_map/ppermute | solution.py:690
  56.8 9.8 %collective-permute-start.10 = (f32[328,128]{1,0:T(8,128)S(1)}, f32[328,128]{1,0:T(8,128)S(1)}, u32[]{:S(2)}, u32[]{:S(2)}) collective-permute-start(f32[328,128]{1,0:T(8,128)S(1)} %get-tuple-element.70), channel_id=1, source_target_pairs={{0,2},{1,3},{2,0},{3,1},{4,6},{5,7},{6,4},{7,5},{8,10},{9,11},{10,... | collective-permute-start | bytes 503816 | tf_op jit(solution)/shard_map/ppermute | solution.py:690
  59.8 6.8 %collective-permute-start.11 = (f32[328,128]{1,0:T(8,128)S(1)}, f32[328,128]{1,0:T(8,128)S(1)}, u32[]{:S(2)}, u32[]{:S(2)}) collective-permute-start(f32[328,128]{1,0:T(8,128)S(1)} %get-tuple-element.71.refs_9_), channel_id=1, source_target_pairs={{0,3},{1,0},{2,1},{3,2},{4,7},{5,4},{6,5},{7,6},{8,11},{9,8},{10,9... | collective-permute-start | bytes 503816 | tf_op jit(solution)/shard_map/ppermute | solution.py:690
  62.0 10.3 %collective-permute-start.18 = (f32[4,8,8,128]{3,2,1,0:T(8,128)S(1)}, f32[4,8,8,128]{3,2,1,0:T(8,128)S(1)}, u32[]{:S(2)}, u32[]{:S(2)}) collective-permute-start(f32[4,8,8,128]{3,2,1,0:T(8,128)S(1)} %get-tuple-element.84), channel_id=1, source_target_pairs={{0,4},{4,0},{8,12},{12,8},{16,20},{20,16},{24,28},{28,24},{32,36},... | collective-permute-start | bytes 393224 | tf_op jit(solution)/shard_map/ppermute | solution.py:698
  66.6 5.7 %collective-permute-start.19 = (f32[4,8,8,128]{3,2,1,0:T(8,128)S(1)}, f32[4,8,8,128]{3,2,1,0:T(8,128)S(1)}, u32[]{:S(2)}, u32[]{:S(2)}) collective-permute-start(f32[4,8,8,128]{3,2,1,0:T(8,128)S(1)} %get-tuple-element.85), channel_id=1, source_target_pairs={{0,124},{4,8},{8,4},{12,16},{16,12},{20,24},{24,20},{28,32},{32,28... | collective-permute-start | bytes 393224 | tf_op jit(solution)/shard_map/ppermute | solution.py:698
  68.0 6.9 %collective-permute-start.16 = (f32[2,8,8,128]{3,2,1,0:T(8,128)S(1)}, f32[2,8,8,128]{3,2,1,0:T(8,128)S(1)}, u32[]{:S(2)}, u32[]{:S(2)}) collective-permute-start(f32[2,8,8,128]{3,2,1,0:T(8,128)S(1)} %get-tuple-element.79), channel_id=1, source_target_pairs={{0,4},{4,0},{8,12},{12,8},{16,20},{20,16},{24,28},{28,24},{32,36},... | collective-permute-start | bytes 196616 | tf_op jit(solution)/shard_map/ppermute | solution.py:698
  72.3 3.7 %collective-permute-start.17 = (f32[2,8,8,128]{3,2,1,0:T(8,128)S(1)}, f32[2,8,8,128]{3,2,1,0:T(8,128)S(1)}, u32[]{:S(2)}, u32[]{:S(2)}) collective-permute-start(f32[2,8,8,128]{3,2,1,0:T(8,128)S(1)} %get-tuple-element.80), channel_id=1, source_target_pairs={{0,124},{4,8},{8,4},{12,16},{16,12},{20,24},{24,20},{28,32},{32,28... | collective-permute-start | bytes 196616 | tf_op jit(solution)/shard_map/ppermute | solution.py:698
  77.6 4.3 %collective-permute-start.20 = (f32[40,128]{1,0:T(8,128)S(1)}, f32[40,128]{1,0:T(8,128)S(1)}, u32[]{:S(2)}, u32[]{:S(2)}) collective-permute-start(f32[40,128]{1,0:T(8,128)S(1)} %get-tuple-element.88.refs_0_.refs_2_), channel_id=1, source_target_pairs={{0,4},{4,0},{8,12},{12,8},{16,20},{20,16},{24,28},{28,24},{32,36},... | collective-permute-start | bytes 61448 | tf_op jit(solution)/shard_map/ppermute | solution.py:835
where the time goes:
time: 96.1 us; the launch traced here: 95.9 us
  starting transfers between devices  36.4 us (38%)
  Pallas kernels  24.8 us (26%)
  waiting for transfers between devices  19.9 us (21%)
  blocking collectives  12.3 us (13%)
  local copies, waits for them, and re-layouts  1.61 us (2%)
    pallas_call x13, Pallas kernels, call(): pl.pallas_call(body, grid=(1,) if grid else (), in_specs=specs, out_specs...  24.8 us
    ppermute x12, starting transfers between devices, swap(): lax.ppermute(blocks[d], 'mode', [(i, (i + d) % GROUPS) for i in range(GRO...  16.8 us
    ppermute x12, waiting for transfers between devices, swap(): lax.ppermute(blocks[d], 'mode', [(i, (i + d) % GROUPS) for i in range(GRO...  14.9 us
    ppermute x4, starting transfers between devices, trade(): lax.ppermute(inner, 'elem', pair)  13.7 us
    all_to_all x1, blocking collectives, on_device(): lax.all_to_all(spread, 'elem', split_axis=0, concat_axis=0, tiled=True, a...  12.3 us
    ppermute x4, waiting for transfers between devices, trade(): lax.ppermute(outer, 'elem', across)  4.16 us
    ppermute x1, starting transfers between devices, on_device(): other = lax.ppermute(total, 'elem', [(i, i ^ 1) for i in range(COLUMNS)])  3.49 us
    ppermute x4, starting transfers between devices, trade(): lax.ppermute(outer, 'elem', across)  2.38 us
  transfers between devices with their start and end apart: 21, of which 8 were waited for; matrix products, arithmetic and copies ran while one was open for 0% of the time, Pallas kernels for 17%

commit v1 on v0

--- a/solution.py
+++ b/solution.py
@@ -44,6 +44,7 @@
 PLANES = 3 * MODES
 HALF = PLANES // 2
 GROUPS = 4
+DISTANCES = (0, 2, 1, 3)
 LOCAL = MODES // GROUPS
 ROWS = 8
 COLUMNS = 32
@@ -186,11 +187,12 @@
     return jnp.where(first, ref[2 * me].astype(F32), ref[2 * me + 1].astype(F32))
 
 
-def load_modes(v_refs, modes_ref, a_ref, b_ref, components):
+def load_modes(v_refs, distances, modes_ref, a_ref, b_ref, components):
     zeros = jnp.zeros((PAD - WIDE, LOCAL), F32)
     extra = jnp.zeros((components * 2 * PAD, LOCAL), F32)
-    for d, v_ref in enumerate(v_refs):
+    for i, (d, v_ref) in enumerate(zip(distances, v_refs)):
         lanes = block_lanes(d)
+        target = pl.ds(i * LOCAL, LOCAL)
         weight = modes_ref[0:1, lanes]
         wave = modes_ref[1:2, lanes]
         a, b = [], []
@@ -201,15 +203,32 @@
             b += [im * weight, zeros, re * wave, zeros]
         a = jnp.concatenate(a, axis=0)
         extra = extra + a * modes_ref[2:3, lanes]
-        a_ref[:, lanes] = split(a)
-        b_ref[:, lanes] = split(jnp.concatenate(b, axis=0))
+        a_ref[:, target] = split(a)
+        b_ref[:, target] = split(jnp.concatenate(b, axis=0))
     return jnp.sum(extra, axis=1, keepdims=True)
 
 
-def plane_values(t, a_ref, b_ref, cos, sin, extra):
+def packed_rows(ref, distances, columns):
+    return jnp.concatenate([ref[block_lanes(d), columns] for d in distances], axis=0)
+
+
+def early_kernel(
+    components, v0_ref, v1_ref, ch_ref, cl_ref, sh_ref, sl_ref, modes_ref,
+    even_ref, odd_ref, extra_ref, a_ref, b_ref,
+):
+    near = DISTANCES[:2]
+    extra = load_modes((v0_ref, v1_ref), near, modes_ref, a_ref, b_ref, components)
+    extra_ref[...] = jnp.broadcast_to(extra, extra_ref.shape)
+    for t in range(HALF // TILE):
+        columns, _ = plane_tile(t)
+        cos = tuple(packed_rows(ref, near, columns) for ref in (ch_ref, cl_ref))
+        sin = tuple(packed_rows(ref, near, columns) for ref in (sh_ref, sl_ref))
+        even_ref[:, columns] = dot3(a_ref[...], cos)
+        odd_ref[:, columns] = dot3(b_ref[...], sin)
+
+
+def plane_values(t, even, odd, extra):
     _, plane = plane_tile(t)
-    even = dot3(a_ref[...], cos)
-    odd = dot3(b_ref[...], sin)
     result = []
     for c in range(extra.shape[0] // (2 * PAD)):
         u = slice(2 * c * PAD, (2 * c + 1) * PAD)
@@ -258,20 +277,24 @@
 
 
 def first_kernel(
-    width_ref, height_ref, disc_ref, v0_ref, v1_ref, v2_ref, v3_ref,
+    width_ref, height_ref, disc_ref, v2_ref, v3_ref, even_ref, odd_ref, extra_ref,
     ch_ref, cl_ref, sh_ref, sl_ref, gradient_ref, modes_ref, nodes_ref,
     field_ref, along_ref, tend_ref, press_ref, a_ref, b_ref,
 ):
-    extra = load_modes((v0_ref, v1_ref, v2_ref, v3_ref), modes_ref, a_ref, b_ref, 2)
+    far = DISTANCES[2:]
+    extra = load_modes((v2_ref, v3_ref), far, modes_ref, a_ref, b_ref, 2)
+    extra = extra + extra_ref[:, 0:1]
     scale_x, scale_y = slope_scales(width_ref, height_ref)
     heights = element_values(height_ref)
     weight = element_values(disc_ref) * (width_ref[0] * heights / 4.0) * nodes_ref[:, 0:1]
     press_ref[...] = jnp.zeros_like(press_ref)
     for t in range(HALF // TILE):
         columns, plane = plane_tile(t)
-        cos = (ch_ref[:, columns], cl_ref[:, columns])
-        sin = (sh_ref[:, columns], sl_ref[:, columns])
-        values = plane_values(t, a_ref, b_ref, cos, sin, extra)
+        cos = tuple(packed_rows(ref, far, columns) for ref in (ch_ref, cl_ref))
+        sin = tuple(packed_rows(ref, far, columns) for ref in (sh_ref, sl_ref))
+        even = even_ref[:, columns] + dot3(a_ref[...], cos)
+        odd = odd_ref[:, columns] + dot3(b_ref[...], sin)
+        values = plane_values(t, even, odd, extra)
         for side in range(2):
             push_x = values[0][0][side] * scale_x
             push_y = values[1][0][side] * scale_y
@@ -290,17 +313,23 @@
 
 
 def second_kernel(
-    v0_ref, v1_ref, v2_ref, v3_ref, along01_ref, tend_ref, press_ref,
+    v2_ref, v3_ref, even_ref, odd_ref, extra_ref, along01_ref, tend_ref, press_ref,
     ch_ref, cl_ref, sh_ref, sl_ref, modes_ref,
     field_ref, along_ref, o0_ref, o1_ref, o2_ref, o3_ref, a_ref, b_ref, re_ref, im_ref,
 ):
     out_refs = (o0_ref, o1_ref, o2_ref, o3_ref)
-    extra = load_modes((v0_ref, v1_ref, v2_ref, v3_ref), modes_ref, a_ref, b_ref, 1)
+    far = DISTANCES[2:]
+    extra = load_modes((v2_ref, v3_ref), far, modes_ref, a_ref, b_ref, 1)
+    extra = extra + extra_ref[:, 0:1]
     for t in range(HALF // TILE):
         columns, _ = plane_tile(t)
         cos = (ch_ref[:, columns], cl_ref[:, columns])
         sin = (sh_ref[:, columns], sl_ref[:, columns])
-        ((field, along),) = plane_values(t, a_ref, b_ref, cos, sin, extra)
+        far_cos = tuple(packed_rows(ref, far, columns) for ref in (ch_ref, cl_ref))
+        far_sin = tuple(packed_rows(ref, far, columns) for ref in (sh_ref, sl_ref))
+        even = even_ref[:, columns] + dot3(a_ref[...], far_cos)
+        odd = odd_ref[:, columns] + dot3(b_ref[...], far_sin)
+        ((field, along),) = plane_values(t, even, odd, extra)
         tends = [[None, None], [None, None]]
         for side in range(2):
             field_ref[side, :, columns] = field[side]
@@ -351,7 +380,7 @@
         for p in range(2):
             for e in range(2):
                 rows, start = edge_rows(side, p, e)
-                for d, v_ref in enumerate((v0_ref, v1_ref, v2_ref, v3_ref)):
+                for d, v_ref in zip(DISTANCES, (v0_ref, v1_ref, v2_ref, v3_ref)):
                     edge_ref[rows, block_lanes(d)] = v_ref[pl.ds(2 * start + p, N1, stride=2), :]
                 tend = FORWARD * re_ref[pl.ds(start, N1), :] if p == 0 else (
                     -FORWARD * im_ref[pl.ds(start, N1), :]
@@ -405,7 +434,7 @@
         thrust = -(0.5 * thrust_coef * ORDER) * (total / area) / width * disc
     jacobian = width * heights / 4.0
     for c in range(v_ref.shape[0]):
-        for d, block_ref in enumerate(blocks):
+        for d, block_ref in zip(DISTANCES, blocks):
             source = lax.rem(me + GROUPS - d, GROUPS)
             rows = pl.ds(pl.multiple_of(source * BLOCK, 8), BLOCK)
             t_ref[c, rows, :] = block_ref[pl.ds(c * BLOCK, BLOCK), :]
@@ -686,9 +715,11 @@
 
 
 def swap(blocks):
-    return [blocks[0]] + [
+    return [
         lax.ppermute(blocks[d], "mode", [(i, (i + d) % GROUPS) for i in range(GROUPS)])
-        for d in range(1, GROUPS)
+        if d
+        else blocks[d]
+        for d in DISTANCES
     ]
 
 
@@ -715,9 +746,6 @@
     def values(count):
         return (count, 2, PAD, HALF) if count > 1 else (2, PAD, HALF)
 
-    def rows_scratch(count):
-        return [pltpu.VMEM((count * 4 * PAD, MODES), BF16) for _ in range(2)]
-
     def modes_scratch(count):
         return [pltpu.VMEM((count * PAD, MODES), F32) for _ in range(2)]
 
@@ -730,21 +758,38 @@
         )
         for chunk in chunks
     ]
+    def packed_scratch(count):
+        return [pltpu.VMEM((count * 4 * PAD, 2 * LOCAL), BF16) for _ in range(2)]
+
+    def early(i):
+        count = chunks[i][1]
+        rows = 2 * count * PAD
+        return run.call(
+            functools.partial(early_kernel, count),
+            [None] * 7,
+            [(rows, HALF), (rows, HALF), (rows, 128)],
+            packed_scratch(count),
+            (1e3, 1e3),
+            *sent[i][:2], *planes, modes,
+        )
+
+    early01 = early(0)
     field01, along01, tend01, press = run.call(
         first_kernel,
-        [smem()] * 3 + [None] * 11,
+        [smem()] * 3 + [None] * 12,
         [values(2)] * 3 + [(8, 128)],
-        rows_scratch(2),
+        packed_scratch(2),
         (1e3, 1e3),
-        *geometry, disc_mask, *sent[0], *planes, gradient, modes, nodes,
+        *geometry, disc_mask, *sent[0][2:], *early01, *planes, gradient, modes, nodes,
     )
+    early2 = early(1)
     field2, along2, *back01 = run.call(
         second_kernel,
-        [None] * 12,
+        [None] * 13,
         [values(1)] * 2 + [block(2)] * GROUPS,
-        rows_scratch(1) + modes_scratch(2),
+        packed_scratch(1) + modes_scratch(2),
         (1e3, 1e3),
-        *sent[1], along01, tend01, press, *planes, modes,
+        *sent[1][2:], *early2, along01, tend01, press, *planes, modes,
     )
     back01 = swap(back01)
     spectrum, edges = (PAD, MODES), (40, MODES)

time: 96.1 us -> 93.9 us (0.977)
  waiting for transfers between devices: 19.9 us -> 17.1 us
    ppermute x12, waiting for transfers between devices: 14.9 us -> 12.2 us  [swap(): lax.ppermute(blocks[d], 'mode', [(i, (i + d) % GROUPS) for i in range(GRO...]
    ppermute x12, starting transfers between devices: 16.8 us -> 19.4 us  [swap(): lax.ppermute(blocks[d], 'mode', [(i, (i + d) % GROUPS) for i in range(GRO...]
    ppermute x4, starting transfers between devices: 13.7 us -> 11.6 us  [trade(): lax.ppermute(inner, 'elem', pair)]
    pallas_call x13 -> x15, Pallas kernels: 24.8 us -> 24.9 us  [call(): pl.pallas_call(body, grid=(1,) if grid else (), in_specs=specs, out_specs...]
  transfers between devices with their start and end apart: 21 -> 21, of which waited for: 8 -> 7; matrix products, arithmetic and copies ran while one was open for 0% -> 0% of each run, Pallas kernels for 17% -> 18%
where the time goes in v1:
time: 93.9 us; the launch traced here: 93.8 us
  starting transfers between devices  36.9 us (39%)
  Pallas kernels  24.9 us (27%)
  waiting for transfers between devices  17.1 us (18%)
  blocking collectives  12.4 us (13%)
  local copies, waits for them, and re-layouts  1.61 us (2%)
    pallas_call x15, Pallas kernels, call(): pl.pallas_call(body, grid=(1,) if grid else (), in_specs=specs, out_specs...  24.9 us
    ppermute x12, starting transfers between devices, swap(): lax.ppermute(blocks[d], 'mode', [(i, (i + d) % GROUPS) for i in range(GRO...  19.4 us
    all_to_all x1, blocking collectives, on_device(): lax.all_to_all(spread, 'elem', split_axis=0, concat_axis=0, tiled=True, a...  12.4 us
    ppermute x12, waiting for transfers between devices, swap(): lax.ppermute(blocks[d], 'mode', [(i, (i + d) % GROUPS) for i in range(GRO...  12.2 us
    ppermute x4, starting transfers between devices, trade(): lax.ppermute(inner, 'elem', pair)  11.6 us
    ppermute x4, waiting for transfers between devices, trade(): lax.ppermute(outer, 'elem', across)  4.01 us
    ppermute x1, starting transfers between devices, on_device(): other = lax.ppermute(total, 'elem', [(i, i ^ 1) for i in range(COLUMNS)])  3.49 us
    ppermute x4, starting transfers between devices, trade(): lax.ppermute(outer, 'elem', across)  2.39 us
  transfers between devices with their start and end apart: 21, of which 7 were waited for; matrix products, arithmetic and copies ran while one was open for 0% of the time, Pallas kernels for 18%

profile of v1, /device:TPU:1, one launch (start us, length us, event | category | flops | bytes accessed | tf_op | source)
XLA Modules:
  0.0 93.8 jit_solution(2751756667666980920)
XLA Ops:
  0.0 1.6 %copy-done = f32[3,648,2,128]{3,2,1,0:T(2,128)S(1)} copy-done((f32[3,648,2,128]{3,2,1,0:T(2,128)S(1)}, f32[3,648,2,128]{3,2,1,0:T(2,128)}, u32[]{:S(2)}) %copy-start) | copy-done | bytes 1990680
  1.6 0.1 shard_map.118
  1.7 0.0 copy-start.2
  1.7 0.0 copy-start.3
  1.7 0.0 copy-start.8
  1.7 4.5 %collective-permute-start.2 = (f32[656,128]{1,0:T(8,128)S(1)}, f32[656,128]{1,0:T(8,128)S(1)}, u32[]{:S(2)}, u32[]{:S(2)}) collective-permute-start(f32[656,128]{1,0:T(8,128)S(1)} %get-tuple-element.57), channel_id=1, source_target_pairs={{0,2},{1,3},{2,0},{3,1},{4,6},{5,7},{6,4},{7,5},{8,10},{9,11},{10,... | collective-permute-start | bytes 1007624 | tf_op jit(solution)/shard_map/ppermute | solution.py:719
  6.2 0.7 collective-permute-start
  6.9 1.9 %collective-permute-start.1 = (f32[656,128]{1,0:T(8,128)S(1)}, f32[656,128]{1,0:T(8,128)S(1)}, u32[]{:S(2)}, u32[]{:S(2)}) collective-permute-start(f32[656,128]{1,0:T(8,128)S(1)} %get-tuple-element.55.refs_1_), channel_id=1, source_target_pairs={{0,3},{1,0},{2,1},{3,2},{4,7},{5,4},{6,5},{7,6},{8,11},{9,8},{10,9... | collective-permute-start | bytes 1007624 | tf_op jit(solution)/shard_map/ppermute | solution.py:719
  8.9 0.1 collective-permute-start.5
  9.0 0.6 collective-permute-start.3
  9.6 4.3 %collective-permute-done.2.refs_1_ = f32[656,128]{1,0:T(8,128)S(1)} collective-permute-done((f32[656,128]{1,0:T(8,128)S(1)}, f32[656,128]{1,0:T(8,128)S(1)}, u32[]{:S(2)}, u32[]{:S(2)}) %collective-permute-start.2) | collective-permute-done | bytes 335904 | tf_op jit(solution)/shard_map/ppermute | solution.py:719
  13.9 2.8 %collective-permute-start.4 = (f32[328,128]{1,0:T(8,128)S(1)}, f32[328,128]{1,0:T(8,128)S(1)}, u32[]{:S(2)}, u32[]{:S(2)}) collective-permute-start(f32[328,128]{1,0:T(8,128)S(1)} %get-tuple-element.58.refs_7_), channel_id=1, source_target_pairs={{0,3},{1,0},{2,1},{3,2},{4,7},{5,4},{6,5},{7,6},{8,11},{9,8},{10,9... | collective-permute-start | bytes 503816 | tf_op jit(solution)/shard_map/ppermute | solution.py:719
  17.4 0.0 copy-start.6
  17.4 0.0 copy-start.9
  17.4 0.0 copy-start.10
  17.4 0.0 copy-start.11
  17.4 1.9 %shard_map.120 = (f32[704,768]{1,0:T(8,128)S(1)}, f32[704,768]{1,0:T(8,128)S(1)}, f32[704,128]{1,0:T(8,128)S(1)}) custom-call(f32[656,128]{1,0:T(8,128)S(1)} %get-tuple-element.56.refs_0_, f32[656,128]{1,0:T(8,128)S(1)} %collective-permute-done.2.refs_1_, bf16[512,768]{1,0:T(8,128)(2,1)S(1)} %copy-done.5, bf16[512,768]{1,0:T(8,128)(2,1)S(1)} %copy-done.4, ...), custom_call_target="tpu_custom_call" | custom-call | flops 1000 | bytes 1000 | tf_op jit(solution)/shard_map/pallas_call | solution.py:701
  19.3 3.1 %collective-permute-done.refs_3_ = f32[656,128]{1,0:T(8,128)S(1)} collective-permute-done((f32[656,128]{1,0:T(8,128)S(1)}, f32[656,128]{1,0:T(8,128)S(1)}, u32[]{:S(2)}, u32[]{:S(2)}) %collective-permute-start) | collective-permute-done | bytes 335904 | tf_op jit(solution)/shard_map/ppermute | solution.py:719
  22.5 4.7 %shard_map.121 = (f32[2,2,176,768]{3,2,1,0:T(8,128)S(1)}, f32[2,2,176,768]{3,2,1,0:T(8,128)S(1)}, f32[2,2,176,768]{3,2,1,0:T(8,128)S(1)}, f32[8,128]{1,0:T(8,128)S(1)}) custom-call(f32[1]{0:T(128)S(6)} %copy.13.refs_0_, f32[8]{0:T(128)S(1)} %copy-done.10, s32[8]{0:T(128)S(1)} %copy-done.11, f32[656,128]{1,0:T(8,128)S(1)} %collective-permute-done.refs_3_, ...), custom_call_target="tpu_custom_call" | custom-call | flops 1000 | bytes 1000 | tf_op jit(solution)/shard_map/pallas_call | solution.py:701
  27.2 1.0 %shard_map.122 = (f32[352,768]{1,0:T(8,128)S(1)}, f32[352,768]{1,0:T(8,128)S(1)}, f32[352,128]{1,0:T(8,128)S(1)}) custom-call(f32[328,128]{1,0:T(8,128)S(1)} %get-tuple-element.64.refs_0_.refs_5_, f32[328,128]{1,0:T(8,128)S(1)} %collective-permute-done.5.refs_1_.refs_6_, bf16[512,768]{1,0:T(8,128)(2,1)S(1)} %copy-done.5, bf16[512,768]{1,0:T(8,128)(2,1)S(1)} %copy-done.4, ...), custom_call_target="tpu_custom_call" | custom-call | flops 1000 | bytes 1000 | tf_op jit(solution)/shard_map/pallas_call | solution.py:701
  28.2 0.7 collective-permute-done.3.refs_0_.refs_7_
  29.0 3.6 %shard_map.123 = (f32[2,176,768]{2,1,0:T(8,128)S(1)}, f32[2,176,768]{2,1,0:T(8,128)S(1)}, f32[656,128]{1,0:T(8,128)S(1)}, f32[656,128]{1,0:T(8,128)S(1)}, f32[65...) custom-call(f32[328,128]{1,0:T(8,128)S(1)} %collective-permute-done.3.refs_0_.refs_7_, ...), custom_call_target="tpu_custom_call" | custom-call | flops 1000 | bytes 1000 | tf_op jit(solution)/shard_map/pallas_call | solution.py:701
  32.6 2.1 %collective-permute-start.8 = (f32[656,128]{1,0:T(8,128)S(1)}, f32[656,128]{1,0:T(8,128)S(1)}, u32[]{:S(2)}, u32[]{:S(2)}) collective-permute-start(f32[656,128]{1,0:T(8,128)S(1)} %get-tuple-element.79), channel_id=1, source_target_pairs={{0,2},{1,3},{2,0},{3,1},{4,6},{5,7},{6,4},{7,5},{8,10},{9,11},{10,... | collective-permute-start | bytes 1007624 | tf_op jit(solution)/shard_map/ppermute | solution.py:719
  34.7 1.6 %collective-permute-start.12 = (f32[656,128]{1,0:T(8,128)S(1)}, f32[656,128]{1,0:T(8,128)S(1)}, u32[]{:S(2)}, u32[]{:S(2)}) collective-permute-start(f32[656,128]{1,0:T(8,128)S(1)} %get-tuple-element.85), channel_id=1, source_target_pairs={{0,1},{1,2},{2,3},{3,0},{4,5},{5,6},{6,7},{7,4},{8,9},{9,10},{10,1... | collective-permute-start | bytes 1007624 | tf_op jit(solution)/shard_map/ppermute | solution.py:719
  36.3 1.0 %collective-permute-start.13 = (f32[656,128]{1,0:T(8,128)S(1)}, f32[656,128]{1,0:T(8,128)S(1)}, u32[]{:S(2)}, u32[]{:S(2)}) collective-permute-start(f32[656,128]{1,0:T(8,128)S(1)} %get-tuple-element.74.refs_15_), channel_id=1, source_target_pairs={{0,3},{1,0},{2,1},{3,2},{4,7},{5,4},{6,5},{7,6},{8,11},{9,8},{10,9... | collective-permute-start | bytes 1007624 | tf_op jit(solution)/shard_map/ppermute | solution.py:719
  37.4 3.1 %shard_map.124 = (f32[176,512]{1,0:T(8,128)S(1)}, f32[176,512]{1,0:T(8,128)S(1)}, f32[40,512]{1,0:T(8,128)S(1)}, f32[40,512]{1,0:T(8,128)S(1)}) custom-call(f32[1]{0:T(128)S(6)} %copy.13.refs_0_, f32[8]{0:T(128)S(1)} %copy-done.10, f32[2,2,176,768]{3,2,1,0:T(8,128)S(1)} %get-tuple-element.62.refs_2_, f32[2,176,768]{2,1,0:T(8,128)S(1)} %get-tuple-element.72.refs_3_, ...), custom_call_target="tpu_custom_call" | custom-call | flops 1000 | bytes 1000 | tf_op jit(solution)/shard_map/pallas_call | solution.py:701
  40.5 2.2 %collective-permute-start.6 = (f32[40,512]{1,0:T(8,128)S(1)}, f32[40,512]{1,0:T(8,128)S(1)}, u32[]{:S(2)}, u32[]{:S(2)}) collective-permute-start(f32[40,512]{1,0:T(8,128)S(1)} %get-tuple-element.77), channel_id=1, source_target_pairs={{0,4},{4,0},{8,12},{12,8},{16,20},{20,16},{24,28},{28,24},{32,36},... | collective-permute-start | bytes 245768 | tf_op jit(solution)/shard_map/ppermute | solution.py:729
  42.7 1.2 %collective-permute-start.7 = (f32[40,512]{1,0:T(8,128)S(1)}, f32[40,512]{1,0:T(8,128)S(1)}, u32[]{:S(2)}, u32[]{:S(2)}) collective-permute-start(f32[40,512]{1,0:T(8,128)S(1)} %get-tuple-element.78.refs_6_), channel_id=1, source_target_pairs={{0,124},{4,8},{8,4},{12,16},{16,12},{20,24},{24,20},{28,32},{32,28... | collective-permute-start | bytes 245768 | tf_op jit(solution)/shard_map/ppermute | solution.py:729
  43.9 3.0 %collective-permute-done.7.refs_4_ = f32[40,512]{1,0:T(8,128)S(1)} collective-permute-done((f32[40,512]{1,0:T(8,128)S(1)}, f32[40,512]{1,0:T(8,128)S(1)}, u32[]{:S(2)}, u32[]{:S(2)}) %collective-permute-start.7) | collective-permute-done | bytes 81952 | tf_op jit(solution)/shard_map/ppermute | solution.py:729
  46.9 0.2 shard_map.125
  47.0 4.1 %collective-permute-done.12.refs_6_ = f32[656,128]{1,0:T(8,128)S(1)} collective-permute-done((f32[656,128]{1,0:T(8,128)S(1)}, f32[656,128]{1,0:T(8,128)S(1)}, u32[]{:S(2)}, u32[]{:S(2)}) %collective-permute-start.12) | collective-permute-done | bytes 335904 | tf_op jit(solution)/shard_map/ppermute | solution.py:719
  51.2 0.9 shard_map.126
  52.0 1.3 %collective-permute-start.14 = (f32[4,8,8,128]{3,2,1,0:T(8,128)S(1)}, f32[4,8,8,128]{3,2,1,0:T(8,128)S(1)}, u32[]{:S(2)}, u32[]{:S(2)}) collective-permute-start(f32[4,8,8,128]{3,2,1,0:T(8,128)S(1)} %get-tuple-element.87), channel_id=1, source_target_pairs={{0,4},{4,0},{8,12},{12,8},{16,20},{20,16},{24,28},{28,24},{32,36},... | collective-permute-start | bytes 393224 | tf_op jit(solution)/shard_map/ppermute | solution.py:729
  53.4 1.2 %collective-permute-start.15 = (f32[4,8,8,128]{3,2,1,0:T(8,128)S(1)}, f32[4,8,8,128]{3,2,1,0:T(8,128)S(1)}, u32[]{:S(2)}, u32[]{:S(2)}) collective-permute-start(f32[4,8,8,128]{3,2,1,0:T(8,128)S(1)} %get-tuple-element.88.refs_6_), channel_id=1, source_target_pairs={{0,124},{4,8},{8,4},{12,16},{16,12},{20,24},{24,20},{28,32},{32,28... | collective-permute-start | bytes 393224 | tf_op jit(solution)/shard_map/ppermute | solution.py:729
  54.6 1.3 %collective-permute-start.9 = (f32[328,128]{1,0:T(8,128)S(1)}, f32[328,128]{1,0:T(8,128)S(1)}, u32[]{:S(2)}, u32[]{:S(2)}) collective-permute-start(f32[328,128]{1,0:T(8,128)S(1)} %get-tuple-element.81), channel_id=1, source_target_pairs={{0,2},{1,3},{2,0},{3,1},{4,6},{5,7},{6,4},{7,5},{8,10},{9,11},{10,... | collective-permute-start | bytes 503816 | tf_op jit(solution)/shard_map/ppermute | solution.py:719
  55.8 1.6 %collective-permute-start.10 = (f32[328,128]{1,0:T(8,128)S(1)}, f32[328,128]{1,0:T(8,128)S(1)}, u32[]{:S(2)}, u32[]{:S(2)}) collective-permute-start(f32[328,128]{1,0:T(8,128)S(1)} %get-tuple-element.82), channel_id=1, source_target_pairs={{0,1},{1,2},{2,3},{3,0},{4,5},{5,6},{6,7},{7,4},{8,9},{9,10},{10,1... | collective-permute-start | bytes 503816 | tf_op jit(solution)/shard_map/ppermute | solution.py:719
  57.5 1.0 %collective-permute-start.11 = (f32[328,128]{1,0:T(8,128)S(1)}, f32[328,128]{1,0:T(8,128)S(1)}, u32[]{:S(2)}, u32[]{:S(2)}) collective-permute-start(f32[328,128]{1,0:T(8,128)S(1)} %get-tuple-element.83.refs_9_), channel_id=1, source_target_pairs={{0,3},{1,0},{2,1},{3,2},{4,7},{5,4},{6,5},{7,6},{8,11},{9,8},{10,9... | collective-permute-start | bytes 503816 | tf_op jit(solution)/shard_map/ppermute | solution.py:719
  58.5 2.0 %shard_map.127 = (f32[4,81,8,128]{3,2,1,0:T(8,128)S(1)}, f32[4,81,8,128]{3,2,1,0:T(8,128)S(1)}, f32[4,8,8,128]{3,2,1,0:T(8,128)S(1)}, f32[4,8,8,128]{3,2,1,0:T(8,128)S(1)}, f32[4,2,8,128]{3,2,1,0:T(8,128)S(1)}) custom-call(f32[1]{0:T(128)S(6)} %copy.13.refs_0_, f32[8]{0:T(128)S(1)} %copy-done.10, f32[4,81,8,128]{3,2,1,0:T(8,128)S(1)} %get-tuple-element.86.refs_2_, ...), custom_call_target="tpu_custom_call" | custom-call | flops 1000 | bytes 1000 | tf_op jit(solution)/shard_map/pallas_call | solution.py:701
  60.5 5.1 %collective-permute-start.18 = (f32[4,8,8,128]{3,2,1,0:T(8,128)S(1)}, f32[4,8,8,128]{3,2,1,0:T(8,128)S(1)}, u32[]{:S(2)}, u32[]{:S(2)}) collective-permute-start(f32[4,8,8,128]{3,2,1,0:T(8,128)S(1)} %get-tuple-element.96), channel_id=1, source_target_pairs={{0,4},{4,0},{8,12},{12,8},{16,20},{20,16},{24,28},{28,24},{32,36},... | collective-permute-start | bytes 393224 | tf_op jit(solution)/shard_map/ppermute | solution.py:729
  65.6 1.4 %shard_map.128 = (f32[2,81,8,128]{3,2,1,0:T(8,128)S(1)}, f32[2,81,8,128]{3,2,1,0:T(8,128)S(1)}, f32[2,8,8,128]{3,2,1,0:T(8,128)S(1)}, f32[2,8,8,128]{3,2,1,0:T(8,128)S(1)}, f32[2,2,8,128]{3,2,1,0:T(8,128)S(1)}) custom-call(f32[1]{0:T(128)S(6)} %copy.13.refs_0_, f32[8]{0:T(128)S(1)} %copy-done.10, f32[3,1296,128]{2,1,0:T(8,128)S(1)} %bitcast.5, ...), custom_call_target="tpu_custom_call" | custom-call | flops 1000 | bytes 1000 | tf_op jit(solution)/shard_map/pallas_call | solution.py:701
  67.0 3.0 %collective-permute-start.16 = (f32[2,8,8,128]{3,2,1,0:T(8,128)S(1)}, f32[2,8,8,128]{3,2,1,0:T(8,128)S(1)}, u32[]{:S(2)}, u32[]{:S(2)}) collective-permute-start(f32[2,8,8,128]{3,2,1,0:T(8,128)S(1)} %get-tuple-element.91), channel_id=1, source_target_pairs={{0,4},{4,0},{8,12},{12,8},{16,20},{20,16},{24,28},{28,24},{32,36},... | collective-permute-start | bytes 196616 | tf_op jit(solution)/shard_map/ppermute | solution.py:729
  70.0 2.6 %shard_map.129 = (f32[4,81,8,128]{3,2,1,0:T(8,128)S(1)}, f32[40,128]{1,0:T(8,128)S(1)}) custom-call(f32[1]{0:T(128)S(6)} %copy.13.refs_0_, f32[8]{0:T(128)S(1)} %copy-done.10, f32[4,81,8,128]{3,2,1,0:T(8,128)S(1)} %get-tuple-element.95.refs_2_, f32[4,8,8,128]{3,2,1,0:T(8,128)S(1)} %collective-permute-done.18.refs_3_, ...), custom_call_target="tpu_custom_call" | custom-call | flops 1000 | bytes 1000 | tf_op jit(solution)/shard_map/pallas_call | solution.py:701
  72.7 1.0 %collective-permute-done.17.refs_4_ = f32[2,8,8,128]{3,2,1,0:T(8,128)S(1)} collective-permute-done((f32[2,8,8,128]{3,2,1,0:T(8,128)S(1)}, f32[2,8,8,128]{3,2,1,0:T(8,128)S(1)}, u32[]{:S(2)}, u32[]{:S(2)}) %collective-permute-start.17) | collective-permute-done | bytes 65568 | tf_op jit(solution)/shard_map/ppermute | solution.py:729
  73.7 1.6 %shard_map.130 = (f32[2,81,8,128]{3,2,1,0:T(8,128)S(1)}, f32[40,128]{1,0:T(8,128)S(1)}) custom-call(f32[1]{0:T(128)S(6)} %copy.13.refs_0_, f32[8]{0:T(128)S(1)} %copy-done.10, f32[2,81,8,128]{3,2,1,0:T(8,128)S(1)} %get-tuple-element.90.refs_2_, f32[2,8,8,128]{3,2,1,0:T(8,128)S(1)} %collective-permute-done.16.refs_3_, ...), custom_call_target="tpu_custom_call" | custom-call | flops 1000 | bytes 1000 | tf_op jit(solution)/shard_map/pallas_call | solution.py:701
  75.3 3.5 %collective-permute-start.20 = (f32[40,128]{1,0:T(8,128)S(1)}, f32[40,128]{1,0:T(8,128)S(1)}, u32[]{:S(2)}, u32[]{:S(2)}) collective-permute-start(f32[40,128]{1,0:T(8,128)S(1)} %get-tuple-element.100.refs_0_.refs_2_), channel_id=1, source_target_pairs={{0,4},{4,0},{8,12},{12,8},{16,20},{20,16},{24,28},{28,24},{32,36},... | collective-permute-start | bytes 61448 | tf_op jit(solution)/shard_map/ppermute | solution.py:880
  78.8 0.8 collective-permute-done.20.refs_1_
  79.7 12.4 %all_to_all.5.refs_1_ = f32[16,40,128]{2,1,0:T(8,128)S(1)} all-to-all(f32[16,40,128]{2,1,0:T(8,128)S(1)} %shard_map.131.refs_6_), channel_id=1, replica_groups={{0,8,16,24,32,40,48,56,64,72,80,88,96,104,112,120},{4,12,20,28,36,44,52..., dimensions={0} | all-to-all | bytes 655360 | tf_op jit(solution)/shard_map/all_to_all | solution.py:884
  92.1 1.7 %shard_map.132 = f32[3,1296,128]{2,1,0:T(8,128)} custom-call(f32[40,128]{1,0:T(8,128)S(1)} %get-tuple-element.100.refs_0_.refs_2_, f32[16,40,128]{2,1,0:T(8,128)S(1)} %all_to_all.5.refs_1_, f32[4,81,8,128]{3,2,1,0:T(8,128)S(1)} %get-tuple-element.98.refs_5_.refs_2_, f32[4,81,8,128]{3,2,1,0:T(8,128)S(1)} %get-tuple-element.101.refs_3_, ...), custom_call_target="tpu_custom_call" | custom-call | flops 1000 | bytes 1000 | tf_op jit(solution)/shard_map/pallas_call | solution.py:701
  (34 shorter events, 0.2 us)
Async XLA Ops:
  0.0 1.6 %copy-start = (f32[3,648,2,128]{3,2,1,0:T(2,128)S(1)}, f32[3,648,2,128]{3,2,1,0:T(2,128)}, u32[]{:S(2)}) copy-start(f32[3,648,2,128]{3,2,1,0:T(2,128)} %param.12) | copy-start | bytes 5971972
  1.6 15.8 %copy-start.4 = (bf16[512,768]{1,0:T(8,128)(2,1)S(1)}, bf16[512,768]{1,0:T(8,128)(2,1)}, u32[]{:S(2)}) copy-start(bf16[512,768]{1,0:T(8,128)(2,1)} %constant.18.clone.refs_3_.refs_9_.refs_10_) | copy-start | bytes 2359300
  1.6 15.8 %copy-start.5 = (bf16[512,768]{1,0:T(8,128)(2,1)S(1)}, bf16[512,768]{1,0:T(8,128)(2,1)}, u32[]{:S(2)}) copy-start(bf16[512,768]{1,0:T(8,128)(2,1)} %constant.17.clone.refs_2_.refs_8_.refs_9_) | copy-start | bytes 2359300
  1.7 15.7 %copy-start.2 = (bf16[512,768]{1,0:T(8,128)(2,1)S(1)}, bf16[512,768]{1,0:T(8,128)(2,1)}, u32[]{:S(2)}) copy-start(bf16[512,768]{1,0:T(8,128)(2,1)} %constant.20.clone.refs_5_.refs_11_.refs_12_) | copy-start | bytes 2359300
  1.7 15.7 %copy-start.3 = (bf16[512,768]{1,0:T(8,128)(2,1)S(1)}, bf16[512,768]{1,0:T(8,128)(2,1)}, u32[]{:S(2)}) copy-start(bf16[512,768]{1,0:T(8,128)(2,1)} %constant.19.clone.refs_4_.refs_10_.refs_11_) | copy-start | bytes 2359300
  1.7 15.7 %copy-start.8 = (f32[8,512]{1,0:T(8,128)S(1)}, f32[8,512]{1,0:T(8,128)}, u32[]{:S(2)}) copy-start(f32[8,512]{1,0:T(8,128)} %constant.21.clone.refs_6_.refs_13_.refs_12_.refs_14_) | copy-start | bytes 49156
  1.7 12.2 %collective-permute-start.2 = (f32[656,128]{1,0:T(8,128)S(1)}, f32[656,128]{1,0:T(8,128)S(1)}, u32[]{:S(2)}, u32[]{:S(2)}) collective-permute-start(f32[656,128]{1,0:T(8,128)S(1)} %get-tuple-element.57), channel_id=1, source_target_pairs={{0,2},{1,3},{2,0},{3,1},{4,6},{5,7},{6,4},{7,5},{8,10},{9,11},{10,... | collective-permute-start | bytes 1007624 | tf_op jit(solution)/shard_map/ppermute | solution.py:719
  6.2 16.2 %collective-permute-start = (f32[656,128]{1,0:T(8,128)S(1)}, f32[656,128]{1,0:T(8,128)S(1)}, u32[]{:S(2)}, u32[]{:S(2)}) collective-permute-start(f32[656,128]{1,0:T(8,128)S(1)} %get-tuple-element.54), channel_id=1, source_target_pairs={{0,1},{1,2},{2,3},{3,0},{4,5},{5,6},{6,7},{7,4},{8,9},{9,10},{10,1... | collective-permute-start | bytes 1007624 | tf_op jit(solution)/shard_map/ppermute | solution.py:719
  6.9 15.5 %collective-permute-start.1 = (f32[656,128]{1,0:T(8,128)S(1)}, f32[656,128]{1,0:T(8,128)S(1)}, u32[]{:S(2)}, u32[]{:S(2)}) collective-permute-start(f32[656,128]{1,0:T(8,128)S(1)} %get-tuple-element.55.refs_1_), channel_id=1, source_target_pairs={{0,3},{1,0},{2,1},{3,2},{4,7},{5,4},{6,5},{7,6},{8,11},{9,8},{10,9... | collective-permute-start | bytes 1007624 | tf_op jit(solution)/shard_map/ppermute | solution.py:719
  8.9 18.2 %collective-permute-start.5 = (f32[328,128]{1,0:T(8,128)S(1)}, f32[328,128]{1,0:T(8,128)S(1)}, u32[]{:S(2)}, u32[]{:S(2)}) collective-permute-start(f32[328,128]{1,0:T(8,128)S(1)} %get-tuple-element.65), channel_id=1, source_target_pairs={{0,2},{1,3},{2,0},{3,1},{4,6},{5,7},{6,4},{7,5},{8,10},{9,11},{10,... | collective-permute-start | bytes 503816 | tf_op jit(solution)/shard_map/ppermute | solution.py:719
  9.0 19.9 %collective-permute-start.3 = (f32[328,128]{1,0:T(8,128)S(1)}, f32[328,128]{1,0:T(8,128)S(1)}, u32[]{:S(2)}, u32[]{:S(2)}) collective-permute-start(f32[328,128]{1,0:T(8,128)S(1)} %get-tuple-element.63), channel_id=1, source_target_pairs={{0,1},{1,2},{2,3},{3,0},{4,5},{5,6},{6,7},{7,4},{8,9},{9,10},{10,1... | collective-permute-start | bytes 503816 | tf_op jit(solution)/shard_map/ppermute | solution.py:719
  13.9 15.1 %collective-permute-start.4 = (f32[328,128]{1,0:T(8,128)S(1)}, f32[328,128]{1,0:T(8,128)S(1)}, u32[]{:S(2)}, u32[]{:S(2)}) collective-permute-start(f32[328,128]{1,0:T(8,128)S(1)} %get-tuple-element.58.refs_7_), channel_id=1, source_target_pairs={{0,3},{1,0},{2,1},{3,2},{4,7},{5,4},{6,5},{7,6},{8,11},{9,8},{10,9... | collective-permute-start | bytes 503816 | tf_op jit(solution)/shard_map/ppermute | solution.py:719
  17.4 5.1 %copy-start.6 = (bf16[704,176]{1,0:T(8,128)(2,1)S(1)}, bf16[704,176]{1,0:T(8,128)(2,1)}, u32[]{:S(2)}) copy-start(bf16[704,176]{1,0:T(8,128)(2,1)} %constant.23.clone.refs_12_.refs_13_) | copy-start | bytes 743428
  17.4 5.1 %copy-start.9 = (f32[176,128]{1,0:T(8,128)S(1)}, f32[176,128]{1,0:T(8,128)}, u32[]{:S(2)}) copy-start(f32[176,128]{1,0:T(8,128)} %constant.22.clone.refs_14_) | copy-start | bytes 270340
  17.4 5.1 %copy-start.10 = (f32[8]{0:T(128)S(1)}, f32[8]{0:T(128)}, u32[]{:S(2)}) copy-start(f32[8]{0:T(128)} %refs_1_.13) | copy-start | bytes 100
  17.4 5.1 %copy-start.11 = (s32[8]{0:T(128)S(1)}, s32[8]{0:T(128)}, u32[]{:S(2)}) copy-start(s32[8]{0:T(128)} %refs_2_.5) | copy-start | bytes 100
  32.6 14.3 %collective-permute-start.8 = (f32[656,128]{1,0:T(8,128)S(1)}, f32[656,128]{1,0:T(8,128)S(1)}, u32[]{:S(2)}, u32[]{:S(2)}) collective-permute-start(f32[656,128]{1,0:T(8,128)S(1)} %get-tuple-element.79), channel_id=1, source_target_pairs={{0,2},{1,3},{2,0},{3,1},{4,6},{5,7},{6,4},{7,5},{8,10},{9,11},{10,... | collective-permute-start | bytes 1007624 | tf_op jit(solution)/shard_map/ppermute | solution.py:719
  34.7 16.5 %collective-permute-start.12 = (f32[656,128]{1,0:T(8,128)S(1)}, f32[656,128]{1,0:T(8,128)S(1)}, u32[]{:S(2)}, u32[]{:S(2)}) collective-permute-start(f32[656,128]{1,0:T(8,128)S(1)} %get-tuple-element.85), channel_id=1, source_target_pairs={{0,1},{1,2},{2,3},{3,0},{4,5},{5,6},{6,7},{7,4},{8,9},{9,10},{10,1... | collective-permute-start | bytes 1007624 | tf_op jit(solution)/shard_map/ppermute | solution.py:719
  36.3 14.8 %collective-permute-start.13 = (f32[656,128]{1,0:T(8,128)S(1)}, f32[656,128]{1,0:T(8,128)S(1)}, u32[]{:S(2)}, u32[]{:S(2)}) collective-permute-start(f32[656,128]{1,0:T(8,128)S(1)} %get-tuple-element.74.refs_15_), channel_id=1, source_target_pairs={{0,3},{1,0},{2,1},{3,2},{4,7},{5,4},{6,5},{7,6},{8,11},{9,8},{10,9... | collective-permute-start | bytes 1007624 | tf_op jit(solution)/shard_map/ppermute | solution.py:719
  37.4 13.8 %copy-start.1 = (f32[3,648,2,128]{3,2,1,0:T(2,128)S(1)}, f32[3,648,2,128]{3,2,1,0:T(2,128)}, u32[]{:S(2)}) copy-start(f32[3,648,2,128]{3,2,1,0:T(2,128)} %param.12) | copy-start | bytes 5971972
  37.4 13.8 %copy-start.7 = (f32[4,8,128]{2,1,0:T(8,128)S(1)}, f32[4,8,128]{2,1,0:T(8,128)}, u32[]{:S(2)}) copy-start(f32[4,8,128]{2,1,0:T(8,128)} %constant.16.clone.refs_8_.refs_5_.refs_7_) | copy-start | bytes 49156
  40.5 3.4 %collective-permute-start.6 = (f32[40,512]{1,0:T(8,128)S(1)}, f32[40,512]{1,0:T(8,128)S(1)}, u32[]{:S(2)}, u32[]{:S(2)}) collective-permute-start(f32[40,512]{1,0:T(8,128)S(1)} %get-tuple-element.77), channel_id=1, source_target_pairs={{0,4},{4,0},{8,12},{12,8},{16,20},{20,16},{24,28},{28,24},{32,36},... | collective-permute-start | bytes 245768 | tf_op jit(solution)/shard_map/ppermute | solution.py:729
  42.7 4.2 %collective-permute-start.7 = (f32[40,512]{1,0:T(8,128)S(1)}, f32[40,512]{1,0:T(8,128)S(1)}, u32[]{:S(2)}, u32[]{:S(2)}) collective-permute-start(f32[40,512]{1,0:T(8,128)S(1)} %get-tuple-element.78.refs_6_), channel_id=1, source_target_pairs={{0,124},{4,8},{8,4},{12,16},{16,12},{20,24},{24,20},{28,32},{32,28... | collective-permute-start | bytes 245768 | tf_op jit(solution)/shard_map/ppermute | solution.py:729
  52.0 6.5 %collective-permute-start.14 = (f32[4,8,8,128]{3,2,1,0:T(8,128)S(1)}, f32[4,8,8,128]{3,2,1,0:T(8,128)S(1)}, u32[]{:S(2)}, u32[]{:S(2)}) collective-permute-start(f32[4,8,8,128]{3,2,1,0:T(8,128)S(1)} %get-tuple-element.87), channel_id=1, source_target_pairs={{0,4},{4,0},{8,12},{12,8},{16,20},{20,16},{24,28},{28,24},{32,36},... | collective-permute-start | bytes 393224 | tf_op jit(solution)/shard_map/ppermute | solution.py:729
  53.4 5.2 %collective-permute-start.15 = (f32[4,8,8,128]{3,2,1,0:T(8,128)S(1)}, f32[4,8,8,128]{3,2,1,0:T(8,128)S(1)}, u32[]{:S(2)}, u32[]{:S(2)}) collective-permute-start(f32[4,8,8,128]{3,2,1,0:T(8,128)S(1)} %get-tuple-element.88.refs_6_), channel_id=1, source_target_pairs={{0,124},{4,8},{8,4},{12,16},{16,12},{20,24},{24,20},{28,32},{32,28... | collective-permute-start | bytes 393224 | tf_op jit(solution)/shard_map/ppermute | solution.py:729
  54.6 11.0 %collective-permute-start.9 = (f32[328,128]{1,0:T(8,128)S(1)}, f32[328,128]{1,0:T(8,128)S(1)}, u32[]{:S(2)}, u32[]{:S(2)}) collective-permute-start(f32[328,128]{1,0:T(8,128)S(1)} %get-tuple-element.81), channel_id=1, source_target_pairs={{0,2},{1,3},{2,0},{3,1},{4,6},{5,7},{6,4},{7,5},{8,10},{9,11},{10,... | collective-permute-start | bytes 503816 | tf_op jit(solution)/shard_map/ppermute | solution.py:719
  55.8 9.7 %collective-permute-start.10 = (f32[328,128]{1,0:T(8,128)S(1)}, f32[328,128]{1,0:T(8,128)S(1)}, u32[]{:S(2)}, u32[]{:S(2)}) collective-permute-start(f32[328,128]{1,0:T(8,128)S(1)} %get-tuple-element.82), channel_id=1, source_target_pairs={{0,1},{1,2},{2,3},{3,0},{4,5},{5,6},{6,7},{7,4},{8,9},{9,10},{10,1... | collective-permute-start | bytes 503816 | tf_op jit(solution)/shard_map/ppermute | solution.py:719
  57.5 8.1 %collective-permute-start.11 = (f32[328,128]{1,0:T(8,128)S(1)}, f32[328,128]{1,0:T(8,128)S(1)}, u32[]{:S(2)}, u32[]{:S(2)}) collective-permute-start(f32[328,128]{1,0:T(8,128)S(1)} %get-tuple-element.83.refs_9_), channel_id=1, source_target_pairs={{0,3},{1,0},{2,1},{3,2},{4,7},{5,4},{6,5},{7,6},{8,11},{9,8},{10,9... | collective-permute-start | bytes 503816 | tf_op jit(solution)/shard_map/ppermute | solution.py:719
  60.5 9.5 %collective-permute-start.18 = (f32[4,8,8,128]{3,2,1,0:T(8,128)S(1)}, f32[4,8,8,128]{3,2,1,0:T(8,128)S(1)}, u32[]{:S(2)}, u32[]{:S(2)}) collective-permute-start(f32[4,8,8,128]{3,2,1,0:T(8,128)S(1)} %get-tuple-element.96), channel_id=1, source_target_pairs={{0,4},{4,0},{8,12},{12,8},{16,20},{20,16},{24,28},{28,24},{32,36},... | collective-permute-start | bytes 393224 | tf_op jit(solution)/shard_map/ppermute | solution.py:729
  65.6 4.5 %collective-permute-start.19 = (f32[4,8,8,128]{3,2,1,0:T(8,128)S(1)}, f32[4,8,8,128]{3,2,1,0:T(8,128)S(1)}, u32[]{:S(2)}, u32[]{:S(2)}) collective-permute-start(f32[4,8,8,128]{3,2,1,0:T(8,128)S(1)} %get-tuple-element.97), channel_id=1, source_target_pairs={{0,124},{4,8},{8,4},{12,16},{16,12},{20,24},{24,20},{28,32},{32,28... | collective-permute-start | bytes 393224 | tf_op jit(solution)/shard_map/ppermute | solution.py:729
  67.0 5.7 %collective-permute-start.16 = (f32[2,8,8,128]{3,2,1,0:T(8,128)S(1)}, f32[2,8,8,128]{3,2,1,0:T(8,128)S(1)}, u32[]{:S(2)}, u32[]{:S(2)}) collective-permute-start(f32[2,8,8,128]{3,2,1,0:T(8,128)S(1)} %get-tuple-element.91), channel_id=1, source_target_pairs={{0,4},{4,0},{8,12},{12,8},{16,20},{20,16},{24,28},{28,24},{32,36},... | collective-permute-start | bytes 196616 | tf_op jit(solution)/shard_map/ppermute | solution.py:729
  70.0 3.7 %collective-permute-start.17 = (f32[2,8,8,128]{3,2,1,0:T(8,128)S(1)}, f32[2,8,8,128]{3,2,1,0:T(8,128)S(1)}, u32[]{:S(2)}, u32[]{:S(2)}) collective-permute-start(f32[2,8,8,128]{3,2,1,0:T(8,128)S(1)} %get-tuple-element.92), channel_id=1, source_target_pairs={{0,124},{4,8},{8,4},{12,16},{16,12},{20,24},{24,20},{28,32},{32,28... | collective-permute-start | bytes 196616 | tf_op jit(solution)/shard_map/ppermute | solution.py:729
  75.3 4.3 %collective-permute-start.20 = (f32[40,128]{1,0:T(8,128)S(1)}, f32[40,128]{1,0:T(8,128)S(1)}, u32[]{:S(2)}, u32[]{:S(2)}) collective-permute-start(f32[40,128]{1,0:T(8,128)S(1)} %get-tuple-element.100.refs_0_.refs_2_), channel_id=1, source_target_pairs={{0,4},{4,0},{8,12},{12,8},{16,20},{20,16},{24,28},{28,24},{32,36},... | collective-permute-start | bytes 61448 | tf_op jit(solution)/shard_map/ppermute | solution.py:880

commit v2 on v1

--- a/solution.py
+++ b/solution.py
@@ -169,9 +169,11 @@
             target = lax.rem(me + d, GROUPS)
             for e in range(2):
                 base = c * BLOCK + e * ELEM_ROWS
-                out_refs[d][pl.ds(base, 2 * NN), :] = v_ref[
-                    c, pl.ds((2 * target + e) * 2 * NN, 2 * NN), :
-                ]
+                start = (2 * target + e) * 2 * NN
+                for offset, count in ((0, 160), (2 * NN - 8, 8)):
+                    out_refs[d][pl.ds(base + offset, count), :] = v_ref[
+                        c, pl.ds(start + offset, count), :
+                    ]
                 out_refs[d][pl.ds(base + 2 * NN, 2), :] = jnp.zeros((2, LOCAL), F32)
 
 

time: 93.9 us -> 93.9 us (level)
  no operation moved by 1% of the time
where the time goes in v2:
time: 93.9 us; the launch traced here: 93.8 us
  starting transfers between devices  36.9 us (39%)
  Pallas kernels  24.9 us (27%)
  waiting for transfers between devices  17 us (18%)
  blocking collectives  12.4 us (13%)
  local copies, waits for them, and re-layouts  1.61 us (2%)
    pallas_call x15, Pallas kernels, call(): pl.pallas_call(body, grid=(1,) if grid else (), in_specs=specs, out_specs...  24.9 us
    ppermute x12, starting transfers between devices, swap(): lax.ppermute(blocks[d], 'mode', [(i, (i + d) % GROUPS) for i in range(GRO...  19.4 us
    all_to_all x1, blocking collectives, on_device(): lax.all_to_all(spread, 'elem', split_axis=0, concat_axis=0, tiled=True, a...  12.4 us
    ppermute x12, waiting for transfers between devices, swap(): lax.ppermute(blocks[d], 'mode', [(i, (i + d) % GROUPS) for i in range(GRO...  12.2 us
    ppermute x4, starting transfers between devices, trade(): lax.ppermute(inner, 'elem', pair)  11.6 us
    ppermute x4, waiting for transfers between devices, trade(): lax.ppermute(outer, 'elem', across)  4.01 us
    ppermute x1, starting transfers between devices, on_device(): other = lax.ppermute(total, 'elem', [(i, i ^ 1) for i in range(COLUMNS)])  3.49 us
    ppermute x4, starting transfers between devices, trade(): lax.ppermute(outer, 'elem', across)  2.39 us
  transfers between devices with their start and end apart: 21, of which 7 were waited for; matrix products, arithmetic and copies ran while one was open for 0% of the time, Pallas kernels for 18%

profile of v2, /device:TPU:1, one launch (start us, length us, event | category | flops | bytes accessed | tf_op | source)
XLA Modules:
  0.0 93.8 jit_solution(3355149536270816246)
XLA Ops:
  0.0 1.6 %copy-done = f32[3,648,2,128]{3,2,1,0:T(2,128)S(1)} copy-done((f32[3,648,2,128]{3,2,1,0:T(2,128)S(1)}, f32[3,648,2,128]{3,2,1,0:T(2,128)}, u32[]{:S(2)}) %copy-start) | copy-done | bytes 1990680
  1.6 0.1 shard_map.118
  1.7 0.0 copy-start.2
  1.7 0.0 copy-start.3
  1.7 0.0 copy-start.8
  1.7 4.5 %collective-permute-start.2 = (f32[656,128]{1,0:T(8,128)S(1)}, f32[656,128]{1,0:T(8,128)S(1)}, u32[]{:S(2)}, u32[]{:S(2)}) collective-permute-start(f32[656,128]{1,0:T(8,128)S(1)} %get-tuple-element.57), channel_id=1, source_target_pairs={{0,2},{1,3},{2,0},{3,1},{4,6},{5,7},{6,4},{7,5},{8,10},{9,11},{10,... | collective-permute-start | bytes 1007624 | tf_op jit(solution)/shard_map/ppermute | solution.py:721
  6.2 0.7 collective-permute-start
  6.9 1.9 %collective-permute-start.1 = (f32[656,128]{1,0:T(8,128)S(1)}, f32[656,128]{1,0:T(8,128)S(1)}, u32[]{:S(2)}, u32[]{:S(2)}) collective-permute-start(f32[656,128]{1,0:T(8,128)S(1)} %get-tuple-element.55.refs_1_), channel_id=1, source_target_pairs={{0,3},{1,0},{2,1},{3,2},{4,7},{5,4},{6,5},{7,6},{8,11},{9,8},{10,9... | collective-permute-start | bytes 1007624 | tf_op jit(solution)/shard_map/ppermute | solution.py:721
  8.9 0.1 collective-permute-start.5
  9.0 0.6 collective-permute-start.3
  9.6 4.3 %collective-permute-done.2.refs_1_ = f32[656,128]{1,0:T(8,128)S(1)} collective-permute-done((f32[656,128]{1,0:T(8,128)S(1)}, f32[656,128]{1,0:T(8,128)S(1)}, u32[]{:S(2)}, u32[]{:S(2)}) %collective-permute-start.2) | collective-permute-done | bytes 335904 | tf_op jit(solution)/shard_map/ppermute | solution.py:721
  13.9 2.8 %collective-permute-start.4 = (f32[328,128]{1,0:T(8,128)S(1)}, f32[328,128]{1,0:T(8,128)S(1)}, u32[]{:S(2)}, u32[]{:S(2)}) collective-permute-start(f32[328,128]{1,0:T(8,128)S(1)} %get-tuple-element.58.refs_7_), channel_id=1, source_target_pairs={{0,3},{1,0},{2,1},{3,2},{4,7},{5,4},{6,5},{7,6},{8,11},{9,8},{10,9... | collective-permute-start | bytes 503816 | tf_op jit(solution)/shard_map/ppermute | solution.py:721
  17.4 0.0 copy-start.6
  17.4 0.0 copy-start.9
  17.4 0.0 copy-start.10
  17.4 0.0 copy-start.11
  17.4 1.9 %shard_map.120 = (f32[704,768]{1,0:T(8,128)S(1)}, f32[704,768]{1,0:T(8,128)S(1)}, f32[704,128]{1,0:T(8,128)S(1)}) custom-call(f32[656,128]{1,0:T(8,128)S(1)} %get-tuple-element.56.refs_0_, f32[656,128]{1,0:T(8,128)S(1)} %collective-permute-done.2.refs_1_, bf16[512,768]{1,0:T(8,128)(2,1)S(1)} %copy-done.5, bf16[512,768]{1,0:T(8,128)(2,1)S(1)} %copy-done.4, ...), custom_call_target="tpu_custom_call" | custom-call | flops 1000 | bytes 1000 | tf_op jit(solution)/shard_map/pallas_call | solution.py:703
  19.3 3.1 %collective-permute-done.refs_3_ = f32[656,128]{1,0:T(8,128)S(1)} collective-permute-done((f32[656,128]{1,0:T(8,128)S(1)}, f32[656,128]{1,0:T(8,128)S(1)}, u32[]{:S(2)}, u32[]{:S(2)}) %collective-permute-start) | collective-permute-done | bytes 335904 | tf_op jit(solution)/shard_map/ppermute | solution.py:721
  22.5 4.7 %shard_map.121 = (f32[2,2,176,768]{3,2,1,0:T(8,128)S(1)}, f32[2,2,176,768]{3,2,1,0:T(8,128)S(1)}, f32[2,2,176,768]{3,2,1,0:T(8,128)S(1)}, f32[8,128]{1,0:T(8,128)S(1)}) custom-call(f32[1]{0:T(128)S(6)} %copy.13.refs_0_, f32[8]{0:T(128)S(1)} %copy-done.10, s32[8]{0:T(128)S(1)} %copy-done.11, f32[656,128]{1,0:T(8,128)S(1)} %collective-permute-done.refs_3_, ...), custom_call_target="tpu_custom_call" | custom-call | flops 1000 | bytes 1000 | tf_op jit(solution)/shard_map/pallas_call | solution.py:703
  27.2 1.0 %shard_map.122 = (f32[352,768]{1,0:T(8,128)S(1)}, f32[352,768]{1,0:T(8,128)S(1)}, f32[352,128]{1,0:T(8,128)S(1)}) custom-call(f32[328,128]{1,0:T(8,128)S(1)} %get-tuple-element.64.refs_0_.refs_5_, f32[328,128]{1,0:T(8,128)S(1)} %collective-permute-done.5.refs_1_.refs_6_, bf16[512,768]{1,0:T(8,128)(2,1)S(1)} %copy-done.5, bf16[512,768]{1,0:T(8,128)(2,1)S(1)} %copy-done.4, ...), custom_call_target="tpu_custom_call" | custom-call | flops 1000 | bytes 1000 | tf_op jit(solution)/shard_map/pallas_call | solution.py:703
  28.2 0.7 collective-permute-done.3.refs_0_.refs_7_
  29.0 3.6 %shard_map.123 = (f32[2,176,768]{2,1,0:T(8,128)S(1)}, f32[2,176,768]{2,1,0:T(8,128)S(1)}, f32[656,128]{1,0:T(8,128)S(1)}, f32[656,128]{1,0:T(8,128)S(1)}, f32[65...) custom-call(f32[328,128]{1,0:T(8,128)S(1)} %collective-permute-done.3.refs_0_.refs_7_, ...), custom_call_target="tpu_custom_call" | custom-call | flops 1000 | bytes 1000 | tf_op jit(solution)/shard_map/pallas_call | solution.py:703
  32.6 2.1 %collective-permute-start.8 = (f32[656,128]{1,0:T(8,128)S(1)}, f32[656,128]{1,0:T(8,128)S(1)}, u32[]{:S(2)}, u32[]{:S(2)}) collective-permute-start(f32[656,128]{1,0:T(8,128)S(1)} %get-tuple-element.79), channel_id=1, source_target_pairs={{0,2},{1,3},{2,0},{3,1},{4,6},{5,7},{6,4},{7,5},{8,10},{9,11},{10,... | collective-permute-start | bytes 1007624 | tf_op jit(solution)/shard_map/ppermute | solution.py:721
  34.7 1.6 %collective-permute-start.12 = (f32[656,128]{1,0:T(8,128)S(1)}, f32[656,128]{1,0:T(8,128)S(1)}, u32[]{:S(2)}, u32[]{:S(2)}) collective-permute-start(f32[656,128]{1,0:T(8,128)S(1)} %get-tuple-element.85), channel_id=1, source_target_pairs={{0,1},{1,2},{2,3},{3,0},{4,5},{5,6},{6,7},{7,4},{8,9},{9,10},{10,1... | collective-permute-start | bytes 1007624 | tf_op jit(solution)/shard_map/ppermute | solution.py:721
  36.3 1.0 %collective-permute-start.13 = (f32[656,128]{1,0:T(8,128)S(1)}, f32[656,128]{1,0:T(8,128)S(1)}, u32[]{:S(2)}, u32[]{:S(2)}) collective-permute-start(f32[656,128]{1,0:T(8,128)S(1)} %get-tuple-element.74.refs_15_), channel_id=1, source_target_pairs={{0,3},{1,0},{2,1},{3,2},{4,7},{5,4},{6,5},{7,6},{8,11},{9,8},{10,9... | collective-permute-start | bytes 1007624 | tf_op jit(solution)/shard_map/ppermute | solution.py:721
  37.4 3.1 %shard_map.124 = (f32[176,512]{1,0:T(8,128)S(1)}, f32[176,512]{1,0:T(8,128)S(1)}, f32[40,512]{1,0:T(8,128)S(1)}, f32[40,512]{1,0:T(8,128)S(1)}) custom-call(f32[1]{0:T(128)S(6)} %copy.13.refs_0_, f32[8]{0:T(128)S(1)} %copy-done.10, f32[2,2,176,768]{3,2,1,0:T(8,128)S(1)} %get-tuple-element.62.refs_2_, f32[2,176,768]{2,1,0:T(8,128)S(1)} %get-tuple-element.72.refs_3_, ...), custom_call_target="tpu_custom_call" | custom-call | flops 1000 | bytes 1000 | tf_op jit(solution)/shard_map/pallas_call | solution.py:703
  40.5 2.2 %collective-permute-start.6 = (f32[40,512]{1,0:T(8,128)S(1)}, f32[40,512]{1,0:T(8,128)S(1)}, u32[]{:S(2)}, u32[]{:S(2)}) collective-permute-start(f32[40,512]{1,0:T(8,128)S(1)} %get-tuple-element.77), channel_id=1, source_target_pairs={{0,4},{4,0},{8,12},{12,8},{16,20},{20,16},{24,28},{28,24},{32,36},... | collective-permute-start | bytes 245768 | tf_op jit(solution)/shard_map/ppermute | solution.py:731
  42.7 1.2 %collective-permute-start.7 = (f32[40,512]{1,0:T(8,128)S(1)}, f32[40,512]{1,0:T(8,128)S(1)}, u32[]{:S(2)}, u32[]{:S(2)}) collective-permute-start(f32[40,512]{1,0:T(8,128)S(1)} %get-tuple-element.78.refs_6_), channel_id=1, source_target_pairs={{0,124},{4,8},{8,4},{12,16},{16,12},{20,24},{24,20},{28,32},{32,28... | collective-permute-start | bytes 245768 | tf_op jit(solution)/shard_map/ppermute | solution.py:731
  43.9 3.0 %collective-permute-done.7.refs_4_ = f32[40,512]{1,0:T(8,128)S(1)} collective-permute-done((f32[40,512]{1,0:T(8,128)S(1)}, f32[40,512]{1,0:T(8,128)S(1)}, u32[]{:S(2)}, u32[]{:S(2)}) %collective-permute-start.7) | collective-permute-done | bytes 81952 | tf_op jit(solution)/shard_map/ppermute | solution.py:731
  46.9 0.2 shard_map.125
  47.0 4.1 %collective-permute-done.12.refs_6_ = f32[656,128]{1,0:T(8,128)S(1)} collective-permute-done((f32[656,128]{1,0:T(8,128)S(1)}, f32[656,128]{1,0:T(8,128)S(1)}, u32[]{:S(2)}, u32[]{:S(2)}) %collective-permute-start.12) | collective-permute-done | bytes 335904 | tf_op jit(solution)/shard_map/ppermute | solution.py:721
  51.2 0.9 shard_map.126
  52.0 1.3 %collective-permute-start.14 = (f32[4,8,8,128]{3,2,1,0:T(8,128)S(1)}, f32[4,8,8,128]{3,2,1,0:T(8,128)S(1)}, u32[]{:S(2)}, u32[]{:S(2)}) collective-permute-start(f32[4,8,8,128]{3,2,1,0:T(8,128)S(1)} %get-tuple-element.87), channel_id=1, source_target_pairs={{0,4},{4,0},{8,12},{12,8},{16,20},{20,16},{24,28},{28,24},{32,36},... | collective-permute-start | bytes 393224 | tf_op jit(solution)/shard_map/ppermute | solution.py:731
  53.4 1.2 %collective-permute-start.15 = (f32[4,8,8,128]{3,2,1,0:T(8,128)S(1)}, f32[4,8,8,128]{3,2,1,0:T(8,128)S(1)}, u32[]{:S(2)}, u32[]{:S(2)}) collective-permute-start(f32[4,8,8,128]{3,2,1,0:T(8,128)S(1)} %get-tuple-element.88.refs_6_), channel_id=1, source_target_pairs={{0,124},{4,8},{8,4},{12,16},{16,12},{20,24},{24,20},{28,32},{32,28... | collective-permute-start | bytes 393224 | tf_op jit(solution)/shard_map/ppermute | solution.py:731
  54.6 1.3 %collective-permute-start.9 = (f32[328,128]{1,0:T(8,128)S(1)}, f32[328,128]{1,0:T(8,128)S(1)}, u32[]{:S(2)}, u32[]{:S(2)}) collective-permute-start(f32[328,128]{1,0:T(8,128)S(1)} %get-tuple-element.81), channel_id=1, source_target_pairs={{0,2},{1,3},{2,0},{3,1},{4,6},{5,7},{6,4},{7,5},{8,10},{9,11},{10,... | collective-permute-start | bytes 503816 | tf_op jit(solution)/shard_map/ppermute | solution.py:721
  55.8 1.6 %collective-permute-start.10 = (f32[328,128]{1,0:T(8,128)S(1)}, f32[328,128]{1,0:T(8,128)S(1)}, u32[]{:S(2)}, u32[]{:S(2)}) collective-permute-start(f32[328,128]{1,0:T(8,128)S(1)} %get-tuple-element.82), channel_id=1, source_target_pairs={{0,1},{1,2},{2,3},{3,0},{4,5},{5,6},{6,7},{7,4},{8,9},{9,10},{10,1... | collective-permute-start | bytes 503816 | tf_op jit(solution)/shard_map/ppermute | solution.py:721
  57.5 1.0 %collective-permute-start.11 = (f32[328,128]{1,0:T(8,128)S(1)}, f32[328,128]{1,0:T(8,128)S(1)}, u32[]{:S(2)}, u32[]{:S(2)}) collective-permute-start(f32[328,128]{1,0:T(8,128)S(1)} %get-tuple-element.83.refs_9_), channel_id=1, source_target_pairs={{0,3},{1,0},{2,1},{3,2},{4,7},{5,4},{6,5},{7,6},{8,11},{9,8},{10,9... | collective-permute-start | bytes 503816 | tf_op jit(solution)/shard_map/ppermute | solution.py:721
  58.5 2.0 %shard_map.127 = (f32[4,81,8,128]{3,2,1,0:T(8,128)S(1)}, f32[4,81,8,128]{3,2,1,0:T(8,128)S(1)}, f32[4,8,8,128]{3,2,1,0:T(8,128)S(1)}, f32[4,8,8,128]{3,2,1,0:T(8,128)S(1)}, f32[4,2,8,128]{3,2,1,0:T(8,128)S(1)}) custom-call(f32[1]{0:T(128)S(6)} %copy.13.refs_0_, f32[8]{0:T(128)S(1)} %copy-done.10, f32[4,81,8,128]{3,2,1,0:T(8,128)S(1)} %get-tuple-element.86.refs_2_, ...), custom_call_target="tpu_custom_call" | custom-call | flops 1000 | bytes 1000 | tf_op jit(solution)/shard_map/pallas_call | solution.py:703
  60.5 5.1 %collective-permute-start.18 = (f32[4,8,8,128]{3,2,1,0:T(8,128)S(1)}, f32[4,8,8,128]{3,2,1,0:T(8,128)S(1)}, u32[]{:S(2)}, u32[]{:S(2)}) collective-permute-start(f32[4,8,8,128]{3,2,1,0:T(8,128)S(1)} %get-tuple-element.96), channel_id=1, source_target_pairs={{0,4},{4,0},{8,12},{12,8},{16,20},{20,16},{24,28},{28,24},{32,36},... | collective-permute-start | bytes 393224 | tf_op jit(solution)/shard_map/ppermute | solution.py:731
  65.6 1.4 %shard_map.128 = (f32[2,81,8,128]{3,2,1,0:T(8,128)S(1)}, f32[2,81,8,128]{3,2,1,0:T(8,128)S(1)}, f32[2,8,8,128]{3,2,1,0:T(8,128)S(1)}, f32[2,8,8,128]{3,2,1,0:T(8,128)S(1)}, f32[2,2,8,128]{3,2,1,0:T(8,128)S(1)}) custom-call(f32[1]{0:T(128)S(6)} %copy.13.refs_0_, f32[8]{0:T(128)S(1)} %copy-done.10, f32[3,1296,128]{2,1,0:T(8,128)S(1)} %bitcast.5, ...), custom_call_target="tpu_custom_call" | custom-call | flops 1000 | bytes 1000 | tf_op jit(solution)/shard_map/pallas_call | solution.py:703
  67.0 3.0 %collective-permute-start.16 = (f32[2,8,8,128]{3,2,1,0:T(8,128)S(1)}, f32[2,8,8,128]{3,2,1,0:T(8,128)S(1)}, u32[]{:S(2)}, u32[]{:S(2)}) collective-permute-start(f32[2,8,8,128]{3,2,1,0:T(8,128)S(1)} %get-tuple-element.91), channel_id=1, source_target_pairs={{0,4},{4,0},{8,12},{12,8},{16,20},{20,16},{24,28},{28,24},{32,36},... | collective-permute-start | bytes 196616 | tf_op jit(solution)/shard_map/ppermute | solution.py:731
  70.0 2.6 %shard_map.129 = (f32[4,81,8,128]{3,2,1,0:T(8,128)S(1)}, f32[40,128]{1,0:T(8,128)S(1)}) custom-call(f32[1]{0:T(128)S(6)} %copy.13.refs_0_, f32[8]{0:T(128)S(1)} %copy-done.10, f32[4,81,8,128]{3,2,1,0:T(8,128)S(1)} %get-tuple-element.95.refs_2_, f32[4,8,8,128]{3,2,1,0:T(8,128)S(1)} %collective-permute-done.18.refs_3_, ...), custom_call_target="tpu_custom_call" | custom-call | flops 1000 | bytes 1000 | tf_op jit(solution)/shard_map/pallas_call | solution.py:703
  72.7 1.0 %collective-permute-done.17.refs_4_ = f32[2,8,8,128]{3,2,1,0:T(8,128)S(1)} collective-permute-done((f32[2,8,8,128]{3,2,1,0:T(8,128)S(1)}, f32[2,8,8,128]{3,2,1,0:T(8,128)S(1)}, u32[]{:S(2)}, u32[]{:S(2)}) %collective-permute-start.17) | collective-permute-done | bytes 65568 | tf_op jit(solution)/shard_map/ppermute | solution.py:731
  73.7 1.6 %shard_map.130 = (f32[2,81,8,128]{3,2,1,0:T(8,128)S(1)}, f32[40,128]{1,0:T(8,128)S(1)}) custom-call(f32[1]{0:T(128)S(6)} %copy.13.refs_0_, f32[8]{0:T(128)S(1)} %copy-done.10, f32[2,81,8,128]{3,2,1,0:T(8,128)S(1)} %get-tuple-element.90.refs_2_, f32[2,8,8,128]{3,2,1,0:T(8,128)S(1)} %collective-permute-done.16.refs_3_, ...), custom_call_target="tpu_custom_call" | custom-call | flops 1000 | bytes 1000 | tf_op jit(solution)/shard_map/pallas_call | solution.py:703
  75.3 3.5 %collective-permute-start.20 = (f32[40,128]{1,0:T(8,128)S(1)}, f32[40,128]{1,0:T(8,128)S(1)}, u32[]{:S(2)}, u32[]{:S(2)}) collective-permute-start(f32[40,128]{1,0:T(8,128)S(1)} %get-tuple-element.100.refs_0_.refs_2_), channel_id=1, source_target_pairs={{0,4},{4,0},{8,12},{12,8},{16,20},{20,16},{24,28},{28,24},{32,36},... | collective-permute-start | bytes 61448 | tf_op jit(solution)/shard_map/ppermute | solution.py:882
  78.8 0.8 collective-permute-done.20.refs_1_
  79.7 12.4 %all_to_all.5.refs_1_ = f32[16,40,128]{2,1,0:T(8,128)S(1)} all-to-all(f32[16,40,128]{2,1,0:T(8,128)S(1)} %shard_map.131.refs_6_), channel_id=1, replica_groups={{0,8,16,24,32,40,48,56,64,72,80,88,96,104,112,120},{4,12,20,28,36,44,52..., dimensions={0} | all-to-all | bytes 655360 | tf_op jit(solution)/shard_map/all_to_all | solution.py:886
  92.1 1.7 %shard_map.132 = f32[3,1296,128]{2,1,0:T(8,128)} custom-call(f32[40,128]{1,0:T(8,128)S(1)} %get-tuple-element.100.refs_0_.refs_2_, f32[16,40,128]{2,1,0:T(8,128)S(1)} %all_to_all.5.refs_1_, f32[4,81,8,128]{3,2,1,0:T(8,128)S(1)} %get-tuple-element.98.refs_5_.refs_2_, f32[4,81,8,128]{3,2,1,0:T(8,128)S(1)} %get-tuple-element.101.refs_3_, ...), custom_call_target="tpu_custom_call" | custom-call | flops 1000 | bytes 1000 | tf_op jit(solution)/shard_map/pallas_call | solution.py:703
  (34 shorter events, 0.2 us)
Async XLA Ops:
  0.0 1.6 %copy-start = (f32[3,648,2,128]{3,2,1,0:T(2,128)S(1)}, f32[3,648,2,128]{3,2,1,0:T(2,128)}, u32[]{:S(2)}) copy-start(f32[3,648,2,128]{3,2,1,0:T(2,128)} %param.12) | copy-start | bytes 5971972
  1.6 15.8 %copy-start.4 = (bf16[512,768]{1,0:T(8,128)(2,1)S(1)}, bf16[512,768]{1,0:T(8,128)(2,1)}, u32[]{:S(2)}) copy-start(bf16[512,768]{1,0:T(8,128)(2,1)} %constant.18.clone.refs_3_.refs_9_.refs_10_) | copy-start | bytes 2359300
  1.6 15.8 %copy-start.5 = (bf16[512,768]{1,0:T(8,128)(2,1)S(1)}, bf16[512,768]{1,0:T(8,128)(2,1)}, u32[]{:S(2)}) copy-start(bf16[512,768]{1,0:T(8,128)(2,1)} %constant.17.clone.refs_2_.refs_8_.refs_9_) | copy-start | bytes 2359300
  1.7 15.7 %copy-start.2 = (bf16[512,768]{1,0:T(8,128)(2,1)S(1)}, bf16[512,768]{1,0:T(8,128)(2,1)}, u32[]{:S(2)}) copy-start(bf16[512,768]{1,0:T(8,128)(2,1)} %constant.20.clone.refs_5_.refs_11_.refs_12_) | copy-start | bytes 2359300
  1.7 15.7 %copy-start.3 = (bf16[512,768]{1,0:T(8,128)(2,1)S(1)}, bf16[512,768]{1,0:T(8,128)(2,1)}, u32[]{:S(2)}) copy-start(bf16[512,768]{1,0:T(8,128)(2,1)} %constant.19.clone.refs_4_.refs_10_.refs_11_) | copy-start | bytes 2359300
  1.7 15.7 %copy-start.8 = (f32[8,512]{1,0:T(8,128)S(1)}, f32[8,512]{1,0:T(8,128)}, u32[]{:S(2)}) copy-start(f32[8,512]{1,0:T(8,128)} %constant.21.clone.refs_6_.refs_13_.refs_12_.refs_14_) | copy-start | bytes 49156
  1.7 12.2 %collective-permute-start.2 = (f32[656,128]{1,0:T(8,128)S(1)}, f32[656,128]{1,0:T(8,128)S(1)}, u32[]{:S(2)}, u32[]{:S(2)}) collective-permute-start(f32[656,128]{1,0:T(8,128)S(1)} %get-tuple-element.57), channel_id=1, source_target_pairs={{0,2},{1,3},{2,0},{3,1},{4,6},{5,7},{6,4},{7,5},{8,10},{9,11},{10,... | collective-permute-start | bytes 1007624 | tf_op jit(solution)/shard_map/ppermute | solution.py:721
  6.2 16.2 %collective-permute-start = (f32[656,128]{1,0:T(8,128)S(1)}, f32[656,128]{1,0:T(8,128)S(1)}, u32[]{:S(2)}, u32[]{:S(2)}) collective-permute-start(f32[656,128]{1,0:T(8,128)S(1)} %get-tuple-element.54), channel_id=1, source_target_pairs={{0,1},{1,2},{2,3},{3,0},{4,5},{5,6},{6,7},{7,4},{8,9},{9,10},{10,1... | collective-permute-start | bytes 1007624 | tf_op jit(solution)/shard_map/ppermute | solution.py:721
  6.9 15.5 %collective-permute-start.1 = (f32[656,128]{1,0:T(8,128)S(1)}, f32[656,128]{1,0:T(8,128)S(1)}, u32[]{:S(2)}, u32[]{:S(2)}) collective-permute-start(f32[656,128]{1,0:T(8,128)S(1)} %get-tuple-element.55.refs_1_), channel_id=1, source_target_pairs={{0,3},{1,0},{2,1},{3,2},{4,7},{5,4},{6,5},{7,6},{8,11},{9,8},{10,9... | collective-permute-start | bytes 1007624 | tf_op jit(solution)/shard_map/ppermute | solution.py:721
  8.9 18.2 %collective-permute-start.5 = (f32[328,128]{1,0:T(8,128)S(1)}, f32[328,128]{1,0:T(8,128)S(1)}, u32[]{:S(2)}, u32[]{:S(2)}) collective-permute-start(f32[328,128]{1,0:T(8,128)S(1)} %get-tuple-element.65), channel_id=1, source_target_pairs={{0,2},{1,3},{2,0},{3,1},{4,6},{5,7},{6,4},{7,5},{8,10},{9,11},{10,... | collective-permute-start | bytes 503816 | tf_op jit(solution)/shard_map/ppermute | solution.py:721
  9.0 19.9 %collective-permute-start.3 = (f32[328,128]{1,0:T(8,128)S(1)}, f32[328,128]{1,0:T(8,128)S(1)}, u32[]{:S(2)}, u32[]{:S(2)}) collective-permute-start(f32[328,128]{1,0:T(8,128)S(1)} %get-tuple-element.63), channel_id=1, source_target_pairs={{0,1},{1,2},{2,3},{3,0},{4,5},{5,6},{6,7},{7,4},{8,9},{9,10},{10,1... | collective-permute-start | bytes 503816 | tf_op jit(solution)/shard_map/ppermute | solution.py:721
  13.9 15.1 %collective-permute-start.4 = (f32[328,128]{1,0:T(8,128)S(1)}, f32[328,128]{1,0:T(8,128)S(1)}, u32[]{:S(2)}, u32[]{:S(2)}) collective-permute-start(f32[328,128]{1,0:T(8,128)S(1)} %get-tuple-element.58.refs_7_), channel_id=1, source_target_pairs={{0,3},{1,0},{2,1},{3,2},{4,7},{5,4},{6,5},{7,6},{8,11},{9,8},{10,9... | collective-permute-start | bytes 503816 | tf_op jit(solution)/shard_map/ppermute | solution.py:721
  17.4 5.1 %copy-start.6 = (bf16[704,176]{1,0:T(8,128)(2,1)S(1)}, bf16[704,176]{1,0:T(8,128)(2,1)}, u32[]{:S(2)}) copy-start(bf16[704,176]{1,0:T(8,128)(2,1)} %constant.23.clone.refs_12_.refs_13_) | copy-start | bytes 743428
  17.4 5.1 %copy-start.9 = (f32[176,128]{1,0:T(8,128)S(1)}, f32[176,128]{1,0:T(8,128)}, u32[]{:S(2)}) copy-start(f32[176,128]{1,0:T(8,128)} %constant.22.clone.refs_14_) | copy-start | bytes 270340
  17.4 5.1 %copy-start.10 = (f32[8]{0:T(128)S(1)}, f32[8]{0:T(128)}, u32[]{:S(2)}) copy-start(f32[8]{0:T(128)} %refs_1_.13) | copy-start | bytes 100
  17.4 5.1 %copy-start.11 = (s32[8]{0:T(128)S(1)}, s32[8]{0:T(128)}, u32[]{:S(2)}) copy-start(s32[8]{0:T(128)} %refs_2_.5) | copy-start | bytes 100
  32.6 14.3 %collective-permute-start.8 = (f32[656,128]{1,0:T(8,128)S(1)}, f32[656,128]{1,0:T(8,128)S(1)}, u32[]{:S(2)}, u32[]{:S(2)}) collective-permute-start(f32[656,128]{1,0:T(8,128)S(1)} %get-tuple-element.79), channel_id=1, source_target_pairs={{0,2},{1,3},{2,0},{3,1},{4,6},{5,7},{6,4},{7,5},{8,10},{9,11},{10,... | collective-permute-start | bytes 1007624 | tf_op jit(solution)/shard_map/ppermute | solution.py:721
  34.7 16.5 %collective-permute-start.12 = (f32[656,128]{1,0:T(8,128)S(1)}, f32[656,128]{1,0:T(8,128)S(1)}, u32[]{:S(2)}, u32[]{:S(2)}) collective-permute-start(f32[656,128]{1,0:T(8,128)S(1)} %get-tuple-element.85), channel_id=1, source_target_pairs={{0,1},{1,2},{2,3},{3,0},{4,5},{5,6},{6,7},{7,4},{8,9},{9,10},{10,1... | collective-permute-start | bytes 1007624 | tf_op jit(solution)/shard_map/ppermute | solution.py:721
  36.3 14.8 %collective-permute-start.13 = (f32[656,128]{1,0:T(8,128)S(1)}, f32[656,128]{1,0:T(8,128)S(1)}, u32[]{:S(2)}, u32[]{:S(2)}) collective-permute-start(f32[656,128]{1,0:T(8,128)S(1)} %get-tuple-element.74.refs_15_), channel_id=1, source_target_pairs={{0,3},{1,0},{2,1},{3,2},{4,7},{5,4},{6,5},{7,6},{8,11},{9,8},{10,9... | collective-permute-start | bytes 1007624 | tf_op jit(solution)/shard_map/ppermute | solution.py:721
  37.4 13.8 %copy-start.1 = (f32[3,648,2,128]{3,2,1,0:T(2,128)S(1)}, f32[3,648,2,128]{3,2,1,0:T(2,128)}, u32[]{:S(2)}) copy-start(f32[3,648,2,128]{3,2,1,0:T(2,128)} %param.12) | copy-start | bytes 5971972
  37.4 13.8 %copy-start.7 = (f32[4,8,128]{2,1,0:T(8,128)S(1)}, f32[4,8,128]{2,1,0:T(8,128)}, u32[]{:S(2)}) copy-start(f32[4,8,128]{2,1,0:T(8,128)} %constant.16.clone.refs_8_.refs_5_.refs_7_) | copy-start | bytes 49156
  40.5 3.4 %collective-permute-start.6 = (f32[40,512]{1,0:T(8,128)S(1)}, f32[40,512]{1,0:T(8,128)S(1)}, u32[]{:S(2)}, u32[]{:S(2)}) collective-permute-start(f32[40,512]{1,0:T(8,128)S(1)} %get-tuple-element.77), channel_id=1, source_target_pairs={{0,4},{4,0},{8,12},{12,8},{16,20},{20,16},{24,28},{28,24},{32,36},... | collective-permute-start | bytes 245768 | tf_op jit(solution)/shard_map/ppermute | solution.py:731
  42.7 4.2 %collective-permute-start.7 = (f32[40,512]{1,0:T(8,128)S(1)}, f32[40,512]{1,0:T(8,128)S(1)}, u32[]{:S(2)}, u32[]{:S(2)}) collective-permute-start(f32[40,512]{1,0:T(8,128)S(1)} %get-tuple-element.78.refs_6_), channel_id=1, source_target_pairs={{0,124},{4,8},{8,4},{12,16},{16,12},{20,24},{24,20},{28,32},{32,28... | collective-permute-start | bytes 245768 | tf_op jit(solution)/shard_map/ppermute | solution.py:731
  52.0 6.5 %collective-permute-start.14 = (f32[4,8,8,128]{3,2,1,0:T(8,128)S(1)}, f32[4,8,8,128]{3,2,1,0:T(8,128)S(1)}, u32[]{:S(2)}, u32[]{:S(2)}) collective-permute-start(f32[4,8,8,128]{3,2,1,0:T(8,128)S(1)} %get-tuple-element.87), channel_id=1, source_target_pairs={{0,4},{4,0},{8,12},{12,8},{16,20},{20,16},{24,28},{28,24},{32,36},... | collective-permute-start | bytes 393224 | tf_op jit(solution)/shard_map/ppermute | solution.py:731
  53.4 5.2 %collective-permute-start.15 = (f32[4,8,8,128]{3,2,1,0:T(8,128)S(1)}, f32[4,8,8,128]{3,2,1,0:T(8,128)S(1)}, u32[]{:S(2)}, u32[]{:S(2)}) collective-permute-start(f32[4,8,8,128]{3,2,1,0:T(8,128)S(1)} %get-tuple-element.88.refs_6_), channel_id=1, source_target_pairs={{0,124},{4,8},{8,4},{12,16},{16,12},{20,24},{24,20},{28,32},{32,28... | collective-permute-start | bytes 393224 | tf_op jit(solution)/shard_map/ppermute | solution.py:731
  54.6 11.0 %collective-permute-start.9 = (f32[328,128]{1,0:T(8,128)S(1)}, f32[328,128]{1,0:T(8,128)S(1)}, u32[]{:S(2)}, u32[]{:S(2)}) collective-permute-start(f32[328,128]{1,0:T(8,128)S(1)} %get-tuple-element.81), channel_id=1, source_target_pairs={{0,2},{1,3},{2,0},{3,1},{4,6},{5,7},{6,4},{7,5},{8,10},{9,11},{10,... | collective-permute-start | bytes 503816 | tf_op jit(solution)/shard_map/ppermute | solution.py:721
  55.8 9.7 %collective-permute-start.10 = (f32[328,128]{1,0:T(8,128)S(1)}, f32[328,128]{1,0:T(8,128)S(1)}, u32[]{:S(2)}, u32[]{:S(2)}) collective-permute-start(f32[328,128]{1,0:T(8,128)S(1)} %get-tuple-element.82), channel_id=1, source_target_pairs={{0,1},{1,2},{2,3},{3,0},{4,5},{5,6},{6,7},{7,4},{8,9},{9,10},{10,1... | collective-permute-start | bytes 503816 | tf_op jit(solution)/shard_map/ppermute | solution.py:721
  57.5 8.1 %collective-permute-start.11 = (f32[328,128]{1,0:T(8,128)S(1)}, f32[328,128]{1,0:T(8,128)S(1)}, u32[]{:S(2)}, u32[]{:S(2)}) collective-permute-start(f32[328,128]{1,0:T(8,128)S(1)} %get-tuple-element.83.refs_9_), channel_id=1, source_target_pairs={{0,3},{1,0},{2,1},{3,2},{4,7},{5,4},{6,5},{7,6},{8,11},{9,8},{10,9... | collective-permute-start | bytes 503816 | tf_op jit(solution)/shard_map/ppermute | solution.py:721
  60.5 9.5 %collective-permute-start.18 = (f32[4,8,8,128]{3,2,1,0:T(8,128)S(1)}, f32[4,8,8,128]{3,2,1,0:T(8,128)S(1)}, u32[]{:S(2)}, u32[]{:S(2)}) collective-permute-start(f32[4,8,8,128]{3,2,1,0:T(8,128)S(1)} %get-tuple-element.96), channel_id=1, source_target_pairs={{0,4},{4,0},{8,12},{12,8},{16,20},{20,16},{24,28},{28,24},{32,36},... | collective-permute-start | bytes 393224 | tf_op jit(solution)/shard_map/ppermute | solution.py:731
  65.6 4.5 %collective-permute-start.19 = (f32[4,8,8,128]{3,2,1,0:T(8,128)S(1)}, f32[4,8,8,128]{3,2,1,0:T(8,128)S(1)}, u32[]{:S(2)}, u32[]{:S(2)}) collective-permute-start(f32[4,8,8,128]{3,2,1,0:T(8,128)S(1)} %get-tuple-element.97), channel_id=1, source_target_pairs={{0,124},{4,8},{8,4},{12,16},{16,12},{20,24},{24,20},{28,32},{32,28... | collective-permute-start | bytes 393224 | tf_op jit(solution)/shard_map/ppermute | solution.py:731
  67.0 5.7 %collective-permute-start.16 = (f32[2,8,8,128]{3,2,1,0:T(8,128)S(1)}, f32[2,8,8,128]{3,2,1,0:T(8,128)S(1)}, u32[]{:S(2)}, u32[]{:S(2)}) collective-permute-start(f32[2,8,8,128]{3,2,1,0:T(8,128)S(1)} %get-tuple-element.91), channel_id=1, source_target_pairs={{0,4},{4,0},{8,12},{12,8},{16,20},{20,16},{24,28},{28,24},{32,36},... | collective-permute-start | bytes 196616 | tf_op jit(solution)/shard_map/ppermute | solution.py:731
  70.0 3.7 %collective-permute-start.17 = (f32[2,8,8,128]{3,2,1,0:T(8,128)S(1)}, f32[2,8,8,128]{3,2,1,0:T(8,128)S(1)}, u32[]{:S(2)}, u32[]{:S(2)}) collective-permute-start(f32[2,8,8,128]{3,2,1,0:T(8,128)S(1)} %get-tuple-element.92), channel_id=1, source_target_pairs={{0,124},{4,8},{8,4},{12,16},{16,12},{20,24},{24,20},{28,32},{32,28... | collective-permute-start | bytes 196616 | tf_op jit(solution)/shard_map/ppermute | solution.py:731
  75.3 4.3 %collective-permute-start.20 = (f32[40,128]{1,0:T(8,128)S(1)}, f32[40,128]{1,0:T(8,128)S(1)}, u32[]{:S(2)}, u32[]{:S(2)}) collective-permute-start(f32[40,128]{1,0:T(8,128)S(1)} %get-tuple-element.100.refs_0_.refs_2_), channel_id=1, source_target_pairs={{0,4},{4,0},{8,12},{12,8},{16,20},{20,16},{24,28},{28,24},{32,36},... | collective-permute-start | bytes 61448 | tf_op jit(solution)/shard_map/ppermute | solution.py:882
